TPU v7x, 128 devices: a whole 4x4x4 slice. The times are simulated.
128 devices in a mesh: dp: 16 (over y, x_hi, core), tensor: 8 (over z, x_lo).
Axes of the slice: x: 4 (x_hi: 2, x_lo: 2; x = x_hi * 2 + x_lo), y: 4, z: 4, core: 2. Of those that a mesh axis runs over, the one named last changes fastest.
Arguments:
- layer_input: bfloat16 [6144, 4096], P('dp', 'tensor'), may hold values from -6 to 6
- w_x: bfloat16 [4096, 4096], P(None, 'tensor'), may hold values from -0.09375 to 0.09375
- gate_in: bfloat16 [6144, 4096], P('dp', 'tensor'), may hold values from -6 to 6
- bc: bfloat16 [6144, 256], P('dp'), may hold values from -4 to 4
- dt_raw: float32 [64, 6144], P('tensor', 'dp'), may hold values from -2.5 to 4.5
- a_log: float32 [64], P('tensor'), may hold values from -6.2 to -2.8
- skip: float32 [64], P('tensor'), may hold values from 0.5 to 1.5
- gain: float32 [4096], P('tensor'), may hold values from 0.5 to 1.5
- doc_ids: int32 [6144], P('dp'), may hold values from 0 to 63, never falling along the last dimension, each value on 1 to 192 neighbouring positions
- d_out: bfloat16 [6144, 4096], P('dp', 'tensor'), may hold values from -6 to 6
- q_prev: float32 [32, 4096], P(None, 'tensor'), may hold values from -6 to 6
- error_in: float32 [65536, 4096], P('dp', 'tensor'), may hold values from -48 to 48
Outputs:
- d_input: bfloat16 [6144, 4096], P('dp', 'tensor')
- d_gate: bfloat16 [6144, 4096], P('dp', 'tensor')
- d_bc: float32 [6144, 256], P('dp')
- d_dt: float32 [64, 6144], P('tensor', 'dp')
- d_alog: float32 [64], P('tensor')
- d_skip: float32 [64], P('tensor')
- d_gain: float32 [4096], P('tensor')
- p_factor: float32 [256, 4096], P('tensor')
- right_factor_mean: float32 [32, 4096], P(None, 'tensor')
- error_out: float32 [65536, 4096], P('dp', 'tensor')
Inputs may be any that keep to these rules, and one draw needn't show every extreme that they name: `doc_ids`: document numbers never fall along the tokens.
All inputs are finite; a program needn't handle non-finite values.
Results may differ from a plain program's by a relative error of at most 0.011.
Values may be sent and summed in bfloat16 or wider, within the bound.
A program may use at most 128 MiB of HBM per device.

v0:
```python
import jax
import jax.numpy as jnp
from jax import lax
from jax.sharding import PartitionSpec as P

EPSILON = 1e-05
HIGH = lax.Precision.HIGHEST


def head_mix(scores, keep_float, keep_mask, inner_head, step_head, decay_head, skip_head):
    step_rates = jnp.exp(decay_head) * step_head
    totals = jnp.cumsum(step_rates)
    decay_spans = totals[None, :] - totals[:, None]
    decays = jnp.exp(jnp.where(keep_mask, decay_spans, 0.0)) * keep_float
    weights = scores * decays * step_head[None, :]
    return jnp.dot(weights, inner_head, precision=HIGH) + skip_head * inner_head


def mix_heads(inner_heads, step_vals, decay_log, skip_gain, state_vals, doc_block):
    state_half = state_vals.shape[1] // 2
    scores = jnp.dot(state_vals[:, state_half:], state_vals[:, :state_half].T, precision=HIGH)
    places = jnp.arange(inner_heads.shape[1], dtype=jnp.int32)
    keep_mask = jnp.logical_and(
        doc_block[:, None] == doc_block[None, :], places[:, None] >= places[None, :]
    )
    keep_float = keep_mask.astype(jnp.float32)

    def one_head(head_parts):
        return head_mix(
            scores,
            keep_float,
            keep_mask,
            head_parts[0],
            head_parts[1],
            head_parts[2],
            head_parts[3],
        )

    return lax.map(jax.checkpoint(one_head), (inner_heads, step_vals, decay_log, skip_gain))


def gram_orthonormal(factor):
    rank_count = factor.shape[1]

    def add_column(column_index, basis):
        column = lax.dynamic_slice_in_dim(factor, column_index, 1, 1)
        for sweep in range(2):
            coefficients = lax.dot_general(basis, column, (((0,), (0,)), ((), ())), precision=HIGH)
            column = column - jnp.dot(basis, coefficients, precision=HIGH)
        column = column / jnp.sqrt(jnp.sum(column * column))
        return lax.dynamic_update_slice_in_dim(basis, column, column_index, 1)

    basis = lax.fori_loop(0, rank_count, add_column, jnp.zeros_like(factor))
    return basis.T


def shards(
    layer_input, w_x, gate_in, bc, dt_raw, a_log, skip, gain, doc_ids, d_out, q_prev, error_in
):
    token_rows = lax.all_gather(layer_input, "tensor", axis=1, tiled=True)
    length = token_rows.shape[0]
    inner_width = w_x.shape[1]
    head_count = a_log.shape[0]
    head_size = inner_width // head_count
    channels = inner_width * lax.axis_size("tensor")
    workers = lax.axis_size("dp")
    inner_vals = jnp.dot(token_rows, w_x, preferred_element_type=jnp.float32).astype(jnp.bfloat16)
    inner_heads = (
        inner_vals.astype(jnp.float32).reshape(length, head_count, head_size).transpose(1, 0, 2)
    )
    step_pos = jax.nn.softplus(dt_raw)

    def forward(heads_in, steps_in, decay_in, skip_in, states_in):
        return mix_heads(heads_in, steps_in, decay_in, skip_in, states_in, doc_ids)

    mixed_heads, pullback = jax.vjp(
        forward, inner_heads, step_pos, a_log, skip, bc.astype(jnp.float32)
    )
    mixed = mixed_heads.transpose(1, 0, 2).reshape(length, inner_width)
    gate_vals = gate_in.astype(jnp.float32)
    gate_sigmoid = jax.nn.sigmoid(gate_vals)
    silu_vals = gate_vals * gate_sigmoid
    gated = mixed * silu_vals
    upstream = d_out.astype(jnp.float32)
    weighted = upstream * gain[None, :]
    square_all, dot_all = lax.psum(
        (jnp.sum(gated * gated, axis=1), jnp.sum(gated * weighted, axis=1)), "tensor"
    )
    row_scale = lax.rsqrt(square_all / channels + EPSILON)
    inner_dot = dot_all / channels
    grad_gated = row_scale[:, None] * weighted - gated * (row_scale**3 * inner_dot)[:, None]
    gain_part = jnp.sum(upstream * gated * row_scale[:, None], axis=0)
    grad_gate = (
        grad_gated * mixed * gate_sigmoid * (1.0 + gate_vals * (1.0 - gate_sigmoid))
    ).astype(jnp.bfloat16)
    grad_mixed = (grad_gated * silu_vals).reshape(length, head_count, head_size).transpose(1, 0, 2)
    grad_heads, grad_steps, grad_decay, grad_skip, state_local = pullback(grad_mixed)
    grad_inner = grad_heads.transpose(1, 0, 2).reshape(length, inner_width).astype(jnp.bfloat16)
    grad_states = lax.psum(state_local, "tensor")
    grad_raw = grad_steps * jax.nn.sigmoid(dt_raw)
    grad_cols = lax.psum_scatter(
        lax.dot_general(
            w_x, grad_inner, (((1,), (1,)), ((), ())), preferred_element_type=jnp.float32
        ),
        "tensor",
        scatter_dimension=0,
        tiled=True,
    )
    grad_rows = grad_cols.T.astype(jnp.bfloat16)
    merged = (
        lax.dot_general(
            token_rows, grad_inner, (((0,), (0,)), ((), ())), preferred_element_type=jnp.float32
        )
        + error_in
    )
    factor = lax.dot_general(merged, q_prev, (((1,), (1,)), ((), ())), precision=HIGH)
    summed_gain, decay_sum, skip_sum = lax.psum((gain_part, grad_decay, grad_skip), "dp")
    factor_sum = lax.psum(factor, "dp")
    factor_mean = factor_sum / workers
    basis_t = gram_orthonormal(factor_mean)
    q_part = lax.dot_general(basis_t, merged, (((1,), (0,)), ((), ())), precision=HIGH)
    right_factor_mean = lax.psum(q_part, "dp") / workers
    error_out = merged - lax.dot_general(
        basis_t, right_factor_mean, (((0,), (0,)), ((), ())), precision=HIGH
    )
    return (
        grad_rows,
        grad_gate,
        grad_states,
        grad_raw,
        decay_sum,
        skip_sum,
        summed_gain,
        basis_t,
        right_factor_mean,
        error_out,
    )


def solution(mesh):
    return jax.shard_map(
        shards,
        mesh=mesh,
        in_specs=(
            P("dp", "tensor"),
            P(None, "tensor"),
            P("dp", "tensor"),
            P("dp", None),
            P("tensor", "dp"),
            P("tensor"),
            P("tensor"),
            P("tensor"),
            P("dp"),
            P("dp", "tensor"),
            P(None, "tensor"),
            P("dp", "tensor"),
        ),
        out_specs=(
            P("dp", "tensor"),
            P("dp", "tensor"),
            P("dp", None),
            P("tensor", "dp"),
            P("tensor"),
            P("tensor"),
            P("tensor"),
            P("tensor", None),
            P(None, "tensor"),
            P("dp", "tensor"),
        ),
        check_vma=False,
    )
```

profile of v0, /device:TPU:1, one launch (start us, length us, event | category | flops | bytes accessed | tf_op | source)
XLA Modules:
  0.0 873.6 jit_solution(793811872457971501)
XLA Ops:
  10.4 8.9 %copy.33 = f32[4096,512]{0,1:T(8,128)} copy(f32[4096,512]{1,0:T(8,128)} %param.29) | data formatting | bytes 16777216 | tf_op args[11]
  19.8 64.5 %all-gather.2.cloned.1.call-done = bf16[384,4096]{1,0:T(8,128)(2,1)} async-done(((bf16[384,512]{1,0:T(8,128)(2,1)}), bf16[384,4096]{1,0:T(8,128)(2,1)}) %all-gather.2.cloned.1.call-update) | async-done | bytes 3145744 | tf_op jit(solution)/shard_map/all_gather | solution.py:60
  84.3 5.8 fusion.45
  90.1 2.3 copy.30
  92.4 40.9 %while.55 = (s32[]{:T(128)}, f32[8,384,64]{1,2,0:T(8,128)S(1)}, f32[8]{0:T(128)S(1)}, f32[8,384]{1,0:T(8,128)S(1)}, f32[384,384]{1,0:T(8,128)S(1)}, /*index=5*/f...) while((s32[]{:T(128)}, f32[8,384,64]{1,2,0:T(8,128)S(1)}, ...), condition=%wide.region_3.4_spmd.clone.clone.clone, body=%wide.region_0.3_spmd.clone.clone.sunk.clone | while | flops 114524552 | bytes 907493 | solution.py:39
  94.9 2.6 fusion.146
  100.0 2.6 fusion.146
  105.1 2.6 fusion.146
  110.3 2.6 fusion.146
  115.4 2.6 fusion.146
  120.5 2.6 fusion.146
  125.6 2.6 fusion.146
  130.7 2.6 fusion.146
  133.6 13.2 %psum.56 = f32[384]{0:T(512)S(1)} all-reduce(f32[384]{0:T(512)S(1)} %multiply_reduce_fusion.4), channel_id=1, replica_groups=mesh['dp'=16,'tensor'=8] {'tensor'}, use_global_device_ids=true, to_apply=%region_5.6 | all-reduce | flops 384 | bytes 3072 | tf_op jit(solution)/shard_map/psum | solution.py:86
  147.3 13.5 %psum.57 = f32[384]{0:T(512)S(1)} all-reduce(f32[384]{0:T(512)S(1)} %get-tuple-element.656), channel_id=1, replica_groups=mesh['dp'=16,'tensor'=8] {'tensor'}, use_global_device_ids=true, to_apply=%region_7.8 | all-reduce | flops 384 | bytes 3072 | tf_op jit(solution)/shard_map/psum | solution.py:86
  160.8 1.5 fusion.57
  162.4 84.1 %while.56 = (s32[]{:T(128)}, f32[384,384]{1,0:T(8,128)S(1)}, bf16[8,384,64]{1,2,0:T(8,128)(2,1)S(1)}, f32[8,384]{1,0:T(8,128)S(1)}, f32[8]{0:T(128)S(1)}, /*inde...) while((s32[]{:T(128)}, f32[384,384]{1,0:T(8,128)S(1)}, ...), condition=%wide.region_18.19_spmd.clone.clone.clone.clone, body=%wide.region_8.18_spmd.clone.clone.clone.sunk.clone | while | flops 230377344 | bytes 6881719 | solution.py:39
  167.4 1.4 fusion.152
  170.0 1.3 reduce-window.93
  177.9 1.4 fusion.152
  180.5 1.3 reduce-window.93
  188.5 1.4 fusion.152
  191.0 1.3 reduce-window.93
  199.0 1.4 fusion.152
  201.5 1.3 reduce-window.93
  209.5 1.4 fusion.152
  212.0 1.3 reduce-window.93
  220.0 1.4 fusion.152
  222.5 1.3 reduce-window.93
  230.5 1.4 fusion.152
  233.0 1.3 reduce-window.93
  241.0 1.4 fusion.152
  243.6 1.3 reduce-window.93
  246.5 6.7 bitcast_add_fusion.1
  253.2 3.4 copy-done.2
  256.6 6.0 fusion.69
  262.9 144.6 %all-reduce.9.cloned.1.call-done = f32[4096,32]{0,1:T(8,128)} async-done(((f32[4096,32]{0,1:T(8,128)}), f32[4096,32]{0,1:T(8,128)}) %all-reduce.9.cloned.1.call-update) | async-done | bytes 524304 | tf_op jit(solution)/shard_map/psum | solution.py:118
  408.6 112.8 %while.54 = (s32[]{:T(128)}, f32[4096,32]{0,1:T(8,128)S(1)}, f32[4096,32]{0,1:T(8,128)S(1)}) while((s32[]{:T(128)}, f32[4096,32]{0,1:T(8,128)S(1)}, f32[4096,32]{0,1:T(8,128)S(1)}) %tuple.146), condition=%wide.region_28.29_spmd.clone, body=%wide.region_26.28_spmd.sunk.clone | while | flops 6311937 | bytes 2261585 | solution.py:53
  521.5 10.8 %fusion.70 = f32[32,512]{1,0:T(8,128)} fusion(f32[4096,32]{0,1:T(8,128)S(1)} %get-tuple-element.445, f32[4096,512]{0,1:T(8,128)} %copy-done.2), kind=kOutput, calls=%fused_computation.116 | convolution fusion | flops 805306368 | bytes 8978432 | tf_op jit(solution)/shard_map/dot_general | solution.py:121
  532.3 6.8 convolution_bitcast_fusion.4
  542.6 34.0 %all-reduce.2 = (f32[8]{0:T(128)}, f32[8]{0:T(128)}, f32[512]{0:T(512)}) all-reduce(f32[8]{0:T(128)S(1)} %get-tuple-element.443, f32[8]{0:T(128)S(1)} %get-tuple-element.444, f32[512]{0:T(512)S(1)} %get-tuple-element.655), channel_id=1, replica_groups=mesh['dp'=16,'tensor'=8] {'dp'}, use_global_device_ids=true, to_apply=%region_21.22 | all-reduce | flops 528 | bytes 4224 | tf_op jit(solution)/shard_map/psum | solution.py:117
  576.6 82.8 %all-reduce.11.cloned.1.call-done = f32[32,512]{1,0:T(8,128)} async-done(((f32[32,512]{1,0:T(8,128)}), f32[32,512]{1,0:T(8,128)}) %all-reduce.11.cloned.1.call-update) | async-done | bytes 65552 | tf_op jit(solution)/shard_map/psum | solution.py:122
  660.2 11.2 %convolution_subtract_fusion = f32[4096,512]{0,1:T(8,128)} fusion(f32[4096,512]{0,1:T(8,128)} %copy-done.2, f32[4096,32]{0,1:T(8,128)S(1)} %get-tuple-element.445, f32[32,512]{1,0:T(8,128)S(1)} %broadcast_multiply_fusion.1), kind=kOutput, calls=%fused_computation.71 | convolution fusion | flops 807403520 | bytes 17367040 | tf_op jit(solution)/shard_map/dot_general | solution.py:123
  671.4 9.0 %copy.36 = f32[4096,512]{1,0:T(8,128)} copy(f32[4096,512]{0,1:T(8,128)} %convolution_subtract_fusion) | data formatting | bytes 16777216
  680.4 110.9 %reduce-scatter.2.cloned.1.call-done = f32[512,384]{0,1:T(8,128)} async-done(((f32[4096,384]{0,1:T(8,128)}), f32[512,384]{0,1:T(8,128)}) %reduce-scatter.2.cloned.1.call-update) | async-done | bytes 786448 | tf_op jit(solution)/shard_map/reduce_scatter | solution.py:101
  791.3 1.9 convert_bitcast_fusion
  793.2 72.1 %all-reduce.7.cloned.1.call-done = f32[384,256]{1,0:T(8,128)} async-done(((f32[384,256]{1,0:T(8,128)}), f32[384,256]{1,0:T(8,128)}) %all-reduce.7.cloned.1.call-update) | async-done | bytes 393232 | tf_op jit(solution)/shard_map/psum | solution.py:99
  865.4 1.8 copy.87
  (493 shorter events, 165.9 us)
Async XLA Ops:
  7.2 249.5 %copy-start = (f32[32,512]{1,0:T(8,128)S(1)}, f32[32,512]{1,0:T(8,128)}, u32[]{:S(2)}) copy-start(f32[32,512]{1,0:T(8,128)} %param.28) | copy-start | bytes 196612
  7.2 77.1 %all-gather.2.cloned.1.call-start = ((), (), s32[]{:S(2)}) async-start(), calls=%async_computation.1 | async-start | bytes 3538944 | tf_op jit(solution)/shard_map/all_gather | solution.py:60
  7.9 399.6 %all-reduce.9.cloned.1.call-start = ((), (), s32[]{:S(2)}) async-start(), calls=%async_computation.4 | async-start | bytes 1048576 | tf_op jit(solution)/shard_map/psum | solution.py:118
  10.4 9.0 %copy-start.7 = (f32[8,384]{1,0:T(8,128)S(1)}, f32[8,384]{1,0:T(8,128)}, u32[]{:S(2)}) copy-start(f32[8,384]{1,0:T(8,128)} %param.22) | copy-start | bytes 36868
  10.4 9.0 %copy-start.4 = (bf16[384,256]{1,0:T(8,128)(2,1)S(1)}, bf16[384,256]{1,0:T(8,128)(2,1)}, u32[]{:S(2)}) copy-start(bf16[384,256]{1,0:T(8,128)(2,1)} %param.21) | copy-start | bytes 589828
  19.7 72.7 %copy-start.6 = (s32[384]{0:T(512)S(1)}, s32[384]{0:T(512)}, u32[]{:S(2)}) copy-start(s32[384]{0:T(512)} %param.26) | copy-start | bytes 4612
  19.7 72.7 %copy-start.9 = (f32[8]{0:T(128)S(1)}, f32[8]{0:T(128)}, u32[]{:S(2)}) copy-start(f32[8]{0:T(128)} %param.23) | copy-start | bytes 100
  19.8 72.6 %copy-start.10 = (f32[8]{0:T(128)S(1)}, f32[8]{0:T(128)}, u32[]{:S(2)}) copy-start(f32[8]{0:T(128)} %param.24) | copy-start | bytes 100
  90.1 56.7 %copy-start.8 = (f32[512]{0:T(512)S(1)}, f32[512]{0:T(512)}, u32[]{:S(2)}) copy-start(f32[512]{0:T(512)} %param.25) | copy-start | bytes 6148
  253.2 3.4 copy-start.2
  262.6 396.7 %all-reduce.11.cloned.1.call-start = ((), (), s32[]{:S(2)}) async-start(), calls=%async_computation.5 | async-start | bytes 131072 | tf_op jit(solution)/shard_map/psum | solution.py:122
  521.5 138.7 %copy-start.1 = (f32[4096,32]{0,1:T(8,128)}, f32[4096,32]{0,1:T(8,128)S(1)}, u32[]{:S(2)}) copy-start(f32[4096,32]{0,1:T(8,128)S(1)} %get-tuple-element.445) | copy-start | bytes 1572868
  532.2 6.9 copy-start.3
  532.3 259.0 %reduce-scatter.2.cloned.1.call-start = ((), (), s32[]{:S(2)}) async-start(), calls=%async_computation.2 | async-start | bytes 7077888 | tf_op jit(solution)/shard_map/reduce_scatter | solution.py:101
  539.1 326.2 %all-reduce.7.cloned.1.call-start = ((), (), s32[]{:S(2)}) async-start(), calls=%async_computation.3 | async-start | bytes 786432 | tf_op jit(solution)/shard_map/psum | solution.py:99
  660.2 11.2 %copy-start.5 = (f32[32,512]{1,0:T(8,128)}, f32[32,512]{1,0:T(8,128)S(1)}, u32[]{:S(2)}) copy-start(f32[32,512]{1,0:T(8,128)S(1)} %broadcast_multiply_fusion.1) | copy-start | bytes 196612
Sparse Core Ops, SparseCore 0:
  9.7 74.5 all-gather.1
  262.7 144.7 all-reduce.8
  532.4 126.9 all-reduce.10
  661.6 129.6 reduce-scatter.1
  794.2 71.1 all-reduce.6
where the time goes:
time: 879 us; the launch traced here: 874 us
  waiting for transfers between devices  476 us (54%)
  matrix products  164 us (19%)
  local copies, waits for them, and re-layouts  79 us (9%)
  blocking collectives  60.7 us (7%)
  loops' own time  40.3 us (5%)
  other arithmetic  39.2 us (4%)
  between operations  14 us (2%)
    psum x1, waiting for transfers between devices, shards(): factor_sum = lax.psum(factor, 'dp')  145 us
    reduce_scatter x1, waiting for transfers between devices, shards(): lax.psum_scatter(lax.dot_general(w_x, grad_inner, (((1,), (1,)), ((), ())...  111 us
    psum x1, waiting for transfers between devices, shards(): right_factor_mean = lax.psum(q_part, 'dp') / workers  82.8 us
    psum x1, waiting for transfers between devices, shards(): grad_states = lax.psum(state_local, 'tensor')  72.1 us
    all_gather x1, waiting for transfers between devices, shards(): token_rows = lax.all_gather(layer_input, 'tensor', axis=1, tiled=True)  64.5 us
    dot_general x64, matrix products, add_column(): column = column - jnp.dot(basis, coefficients, precision=HIGH)  43.4 us
    dot_general x24, matrix products, head_mix(): return jnp.dot(weights, inner_head, precision=HIGH) + skip_head * inner_head  39.5 us
    psum x1, blocking collectives, shards(): lax.psum((gain_part, grad_decay, grad_skip), 'dp')  34 us
  transfers between devices with their start and end apart: 5, of which 5 were waited for; matrix products, arithmetic and copies ran while one was open for 5% of the time, Pallas kernels for 0%

commit v1 on v0

v1 whole, which is shorter than its diff:
```python
import jax
import jax.numpy as jnp
from jax import lax
from jax.experimental import pallas as pl
from jax.experimental.pallas import tpu as pltpu
from jax.sharding import PartitionSpec as P

EPSILON = 1e-05
HIGH = lax.Precision.HIGHEST
MESH = pl.DeviceIdType.MESH
F32 = jnp.float32
BF16 = jnp.bfloat16
T = 384
HALF = T // 2
HEADS = 8
CH = 512
NT = 8
NDP = 16
D = 4096
RANK = 32
BLK = 128
NB = T // BLK
LOW = -1e30
VMEM_LIMIT = 56 * 1024 * 1024


def dot_nn(a, b):
    return lax.dot_general(a, b, (((1,), (0,)), ((), ())), preferred_element_type=F32)


def dot_nt(a, b):
    return lax.dot_general(a, b, (((1,), (1,)), ((), ())), preferred_element_type=F32)


def split2(v):
    hi = v.astype(BF16)
    lo = (v - hi.astype(F32)).astype(BF16)
    return hi, lo


def split3(v):
    hi = v.astype(BF16)
    rest = v - hi.astype(F32)
    mid = rest.astype(BF16)
    lo = (rest - mid.astype(F32)).astype(BF16)
    return hi, mid, lo


def iota(shape, dim):
    return lax.broadcasted_iota(jnp.int32, shape, dim)


def to_column(row):
    return jnp.broadcast_to(row, (BLK, row.shape[1])).T


def head_rates(alog_ref):
    rows = iota((HEADS, T), 0)
    logs = jnp.zeros((HEADS, T), F32)
    for h in range(HEADS):
        logs = jnp.where(rows == h, alog_ref[h], logs)
    return jnp.exp(logs)


def softplus(v):
    return jnp.maximum(v, 0.0) + jnp.log1p(jnp.exp(-jnp.abs(v)))


def keep_bias(doc_ref, bias_ref, bias_t_ref):
    doc_row = doc_ref[...].astype(F32)
    doc_col = to_column(doc_row)
    for i in range(NB):
        for j in range(NB):
            rows = iota((BLK, BLK), 0) + i * BLK
            cols = iota((BLK, BLK), 1) + j * BLK
            same = doc_col[i * BLK : (i + 1) * BLK] == doc_row[:, j * BLK : (j + 1) * BLK]
            spot = (slice(i * BLK, (i + 1) * BLK), slice(j * BLK, (j + 1) * BLK))
            bias_ref[spot] = jnp.where(jnp.logical_and(same, rows >= cols), 0.0, LOW)
            if bias_t_ref is not None:
                bias_t_ref[spot] = jnp.where(jnp.logical_and(same, rows <= cols), 0.0, LOW)


def forward_kernel(
    x_ref, wx_hbm, e_hbm, gate_ref, dout_ref, bc_ref, dt_ref, alog_ref, skip_ref, gain_ref,
    doc_ref, q_ref,
    xall_hbm, eq_ref, inner_ref, dxb_ref, dy_ref, dgate_ref, stat_ref, cum_ref, rowp_ref,
    xall, wx, ebuf, w_mat, wt_mat, cum_col, rowp_col, bias, bias_t, scores, scores_t,
    acc, y_buf, sums, sums_in,
    x_send, x_recv, s_send, s_recv, wx_sem, e_sem, out_sem,
):
    me = lax.axis_index("tensor")
    z = me // 2
    xl = me % 2
    zp = ((z + 1) % 4) * 2 + xl
    zm = ((z + 3) % 4) * 2 + xl
    zo = ((z + 2) % 4) * 2 + xl
    xp = z * 2 + (1 - xl)

    barrier = pltpu.get_barrier_semaphore()
    for k in range(1, NT):
        pl.semaphore_signal(
            barrier, inc=1, device_id={"tensor": (me + k) % NT}, device_id_type=MESH
        )

    def wx_copy(b):
        rows = pl.ds(b * CH, CH)
        return pltpu.make_async_copy(wx_hbm.at[rows], wx.at[rows], wx_sem.at[b])

    def e_copy(b):
        return pltpu.make_async_copy(e_hbm.at[pl.ds(b * CH, CH)], ebuf.at[b % 2], e_sem.at[b % 2])

    e_copy(0).start()
    e_copy(1).start()
    for b in range(NT):
        wx_copy(b).start()

    xall[me] = x_ref[...]
    pl.semaphore_wait(barrier, NT - 1)

    def x_copy(way, to, src, half):
        part = xall.at[src, pl.ds(half * HALF, HALF)]
        return pltpu.make_async_remote_copy(
            src_ref=part,
            dst_ref=part,
            send_sem=x_send.at[way, src, half],
            recv_sem=x_recv.at[src, half],
            device_id={"tensor": to},
            device_id_type=MESH,
        )

    sent = []

    def send(way, to, src, half):
        copy = x_copy(way, to, src, half)
        copy.start()
        sent.append(copy)

    def arrive(src, half):
        x_copy(0, zp, src, half).wait_recv()

    for half in range(2):
        send(0, zp, me, half)
        send(1, zm, me, half)
        send(2, xp, me, half)

    step = softplus(dt_ref[...])
    rate = head_rates(alog_ref) * step
    upper = (iota((T, T), 0) <= iota((T, T), 1)).astype(F32)
    cum = jnp.dot(rate, upper, precision=HIGH, preferred_element_type=F32)
    cum_ref[...] = cum
    rowp_ref[...] = cum + jnp.log(step)
    keep_bias(doc_ref, bias, bias_t)
    b_part = bc_ref[:, :128]
    c_part = bc_ref[:, 128:]
    scores[...] = dot_nt(c_part, b_part)
    scores_t[...] = dot_nt(b_part, c_part)

    q_hi, q_lo = split2(q_ref[...])
    q_two = jnp.concatenate([q_hi, q_lo], axis=0)

    def e_block(b):
        e_copy(b).wait()
        e_hi, e_lo = split2(ebuf[b % 2])
        if b + 2 < NT:
            pass
        both = dot_nt(q_two, e_hi)
        eq_ref[:, b * CH : (b + 1) * CH] = both[:RANK] + both[RANK:] + dot_nt(q_hi, e_lo)
        if b + 2 < NT:
            e_copy(b + 2).start()

    for b in range(NT):
        e_block(b)

    arrive(zm, 0)
    send(0, zp, zm, 0)
    arrive(xp, 0)
    send(0, zp, xp, 0)
    send(1, zm, xp, 0)

    def weights(h, carry):
        cum_row = cum_ref[pl.ds(h, 1), :]
        rowp_row = rowp_ref[pl.ds(h, 1), :]
        col = to_column(cum_row)
        colp = to_column(rowp_row)
        for i in range(NB):
            here = slice(i * BLK, (i + 1) * BLK)
            for j in range(NB):
                there = slice(j * BLK, (j + 1) * BLK)
                if j <= i:
                    span = rowp_row[:, there] - col[here] + bias[here, there]
                    w_mat[h, here, there] = (scores[here, there] * jnp.exp(span)).astype(BF16)
                if j >= i:
                    span = colp[here] - cum_row[:, there] + bias_t[here, there]
                    wt_mat[h, here, there] = (scores_t[here, there] * jnp.exp(span)).astype(BF16)
        return carry

    lax.fori_loop(0, HEADS, weights, 0)

    arrive(zp, 1)
    send(1, zm, zp, 1)
    arrive(xp, 1)
    send(0, zp, xp, 1)
    send(1, zm, xp, 1)

    for b in range(NT):
        wx_copy(b).wait()
    arrive(zm, 1)
    arrive(zp, 0)

    def product(src):
        rows = pl.ds(pl.multiple_of(src * CH, CH), CH)
        return dot_nn(xall[src], wx[rows, :])

    acc[...] = product(me) + product(xp)
    acc[...] += product(zm) + product(zp)
    arrive(zo, 0)
    send(2, xp, zo, 0)
    arrive(zo, 1)
    send(2, xp, zo, 1)
    acc[...] += product(zo)
    xp_zp = ((z + 1) % 4) * 2 + (1 - xl)
    xp_zm = ((z + 3) % 4) * 2 + (1 - xl)
    xp_zo = ((z + 2) % 4) * 2 + (1 - xl)
    for other in (xp_zp, xp_zm, xp_zo):
        arrive(other, 0)
        arrive(other, 1)
        acc[...] += product(other)
    keep = pltpu.make_async_copy(xall, xall_hbm, out_sem)
    keep.start()
    inner_ref[...] = acc[...].astype(BF16)

    low_lanes = iota((1, BLK), 1) < 64

    def pair_lanes(p):
        return pl.ds(pl.multiple_of(p * BLK, BLK), BLK)

    def pair_skip(p):
        return jnp.where(low_lanes, skip_ref[2 * p], skip_ref[2 * p + 1])

    def gate_parts(lanes):
        gate = gate_ref[:, lanes].astype(F32)
        sig = 1.0 / (1.0 + jnp.exp(-gate))
        return gate, sig, gate * sig

    def mix(p, carry):
        square, product_sum = carry
        lanes = pair_lanes(p)
        x_pair = inner_ref[:, lanes]
        for i in range(NB):
            here = slice(i * BLK, (i + 1) * BLK)
            width = (i + 1) * BLK
            first = dot_nn(w_mat[2 * p, here, :width], x_pair[:width])
            second = dot_nn(w_mat[2 * p + 1, here, :width], x_pair[:width])
            y_buf[here, lanes] = jnp.where(low_lanes, first, second) + pair_skip(
                p
            ) * x_pair[here].astype(F32)
        gate, sig, silu = gate_parts(lanes)
        g = y_buf[:, lanes] * silu
        weighted = dout_ref[:, lanes].astype(F32) * gain_ref[:, lanes]
        return square + g * g, product_sum + g * weighted

    zero = jnp.zeros((T, BLK), F32)
    square, product_sum = lax.fori_loop(0, HEADS // 2, mix, (zero, zero))
    sums[0:1, :] = jnp.sum(square.T, axis=0, keepdims=True)
    sums[1:2, :] = jnp.sum(product_sum.T, axis=0, keepdims=True)
    sums[2:8, :] = jnp.zeros((6, T), F32)

    def s_copy(k):
        return pltpu.make_async_remote_copy(
            src_ref=sums,
            dst_ref=sums_in.at[k],
            send_sem=s_send.at[k],
            recv_sem=s_recv.at[k],
            device_id={"tensor": (me + k) % NT},
            device_id_type=MESH,
        )

    for k in range(1, NT):
        s_copy(k).start()
    total = sums[...]
    for k in range(1, NT):
        s_copy(k).wait_recv()
        total = total + sums_in[k]
    r_row = lax.rsqrt(total[0:1] / D + EPSILON)
    r_col = to_column(r_row)
    m_col = to_column(r_row * r_row * r_row * (total[1:2] / D))

    def back(p, carry):
        lanes = pair_lanes(p)
        gate, sig, silu = gate_parts(lanes)
        y = y_buf[:, lanes]
        g = y * silu
        up = dout_ref[:, lanes].astype(F32)
        dg = r_col * (up * gain_ref[:, lanes]) - g * m_col
        dgate_ref[:, lanes] = (dg * y * sig * (1.0 + gate * (1.0 - sig))).astype(BF16)
        dy = dg * silu
        dy_low = dy.astype(BF16)
        dy_ref[:, lanes] = dy_low
        stat_ref[pl.ds(p, 1), :] = jnp.sum(up * g * r_col, axis=0, keepdims=True)
        stat_ref[pl.ds(4 + p, 1), :] = jnp.sum(
            dy * inner_ref[:, lanes].astype(F32), axis=0, keepdims=True
        )
        for i in range(NB):
            here = slice(i * BLK, (i + 1) * BLK)
            first = dot_nn(wt_mat[2 * p, here, i * BLK :], dy_low[i * BLK :])
            second = dot_nn(wt_mat[2 * p + 1, here, i * BLK :], dy_low[i * BLK :])
            dxb_ref[here, lanes] = (
                jnp.where(low_lanes, first, second) + pair_skip(p) * dy[here]
            ).astype(BF16)
        return carry

    lax.fori_loop(0, HEADS // 2, back, 0)
    for copy in sent:
        copy.wait_send()
    for k in range(1, NT):
        s_copy(k).wait_send()
    keep.wait()


def factor_kernel(
    xall_hbm, e_hbm, wx_hbm, eq_ref, dxb_ref, dy_ref, inner_ref, q_ref, bc_ref, cum_ref, rowp_ref,
    dt_ref, doc_ref, alog_ref, stat_ref,
    ph_ref, qm_ref, dinp_ref, dbc_ref, ddt_ref, pay_ref,
    xall, e_all, wx, p_send, p_in, p_own, p_full, d_out, d_in, d_own, b_out, b_in, b_sum,
    bias, scores, d_scores, row_sum, col_sum, pay, pay_in, q_out, q_in, q_own, q_full,
    load_sem, e_sem, ps_sem, pr_sem, gs_sem, gr_sem, ds_sem, dr_sem, bs_sem, br_sem, cs_sem, cr_sem,
    ys_sem, yr_sem, qs_sem, qr_sem, hs_sem, hr_sem,
):
    w = lax.axis_index("dp")
    me = lax.axis_index("tensor")
    barrier = pltpu.get_barrier_semaphore()

    def greet_workers(k, carry):
        pl.semaphore_signal(barrier, inc=1, device_id={"dp": (w + k) % NDP}, device_id_type=MESH)
        return carry

    def greet_shards(k, carry):
        pl.semaphore_signal(barrier, inc=1, device_id={"tensor": (me + k) % NT}, device_id_type=MESH)
        return carry

    lax.fori_loop(1, NDP, greet_workers, 0)
    lax.fori_loop(1, NT, greet_shards, 0)
    x_load = pltpu.make_async_copy(xall_hbm, xall, load_sem.at[0])
    x_load.start()
    wx_load = pltpu.make_async_copy(wx_hbm, wx, load_sem.at[1])
    wx_load.start()
    e_load = pltpu.make_async_copy(e_hbm, e_all, e_sem)
    e_load.start()

    def remote(src, dst, send_sem, recv_sem, axis, to):
        return pltpu.make_async_remote_copy(
            src_ref=src, dst_ref=dst, send_sem=send_sem, recv_sem=recv_sem,
            device_id={axis: to}, device_id_type=MESH,
        )

    def loop(count, body):
        def step(k, carry):
            body(k)
            return carry
        lax.fori_loop(1, count, step, 0)

    dxb = dxb_ref[...]
    q3 = jnp.concatenate(split3(q_ref[...]), axis=0)
    z3 = dot_nt(q3, dxb)
    z_sum = z3[:RANK] + z3[RANK : 2 * RANK] + z3[2 * RANK :]
    z_three = jnp.concatenate(split3(z_sum), axis=0)
    x_load.wait()
    for s in range(NT):
        part = dot_nn(z_three, xall[s])
        part = part[:RANK] + part[RANK : 2 * RANK] + part[2 * RANK :]
        part = part + eq_ref[:, s * CH : (s + 1) * CH]
        p_send[2 * s] = part[:, :256]
        p_send[2 * s + 1] = part[:, 256:]
    pl.semaphore_wait(barrier, NDP - 1 + NT - 1)

    def p_copy(k):
        to = (w + k) % NDP
        return remote(p_send.at[to], p_in.at[k], ps_sem.at[k], pr_sem.at[k], "dp", to)

    loop(NDP, lambda k: p_copy(k).start())

    wx_load.wait()

    def d_copy(k):
        to = (me + k) % NT
        return remote(d_out.at[k], d_in.at[k], ds_sem.at[k], dr_sem.at[k], "tensor", to)

    def input_part(s):
        rows = pl.ds(pl.multiple_of(s * CH, CH), CH)
        return dot_nt(dxb, wx[rows, :])

    def send_input(k):
        d_out[k] = input_part((me + k) % NT).astype(BF16)
        d_copy(k).start()

    loop(NT, send_input)
    d_own[...] = input_part(me)

    keep_bias(doc_ref, bias, None)
    b_part = bc_ref[:, :128]
    c_part = bc_ref[:, 128:]
    scores[...] = dot_nt(c_part, b_part)
    d_scores[...] = jnp.zeros((T, T), F32)
    low_lanes = iota((1, BLK), 1) < 64

    def head_back(p, carry):
        lanes = pl.ds(pl.multiple_of(p * BLK, BLK), BLK)
        x_pair = inner_ref[:, lanes]
        dy_pair = dy_ref[:, lanes]
        for side in range(2):
            h = 2 * p + side
            mine = low_lanes if side == 0 else jnp.logical_not(low_lanes)
            x_mine = jnp.where(mine, x_pair, jnp.zeros_like(x_pair))
            rowp_row = rowp_ref[pl.ds(h, 1), :]
            col = to_column(cum_ref[pl.ds(h, 1), :])
            downs = [jnp.zeros((1, BLK), F32) for _ in range(NB)]
            acrosses = []
            for i in range(NB):
                here = slice(i * BLK, (i + 1) * BLK)
                width = (i + 1) * BLK
                d_weight = dot_nt(dy_pair[here], x_mine[:width])
                across = jnp.zeros((BLK, BLK), F32)
                for j in range(i + 1):
                    there = slice(j * BLK, (j + 1) * BLK)
                    span = rowp_row[:, there] - col[here] + bias[here, there]
                    d_score = d_weight[:, there] * jnp.exp(span)
                    d_scores[here, there] += d_score
                    both = d_score * scores[here, there]
                    downs[j] = downs[j] + jnp.sum(both, axis=0, keepdims=True)
                    across = across + both
                acrosses.append(jnp.sum(across.T, axis=0, keepdims=True))
            col_sum[pl.ds(h, 1), :] = jnp.concatenate(downs, axis=1)
            row_sum[pl.ds(h, 1), :] = jnp.concatenate(acrosses, axis=1)
        return carry

    lax.fori_loop(0, HEADS // 2, head_back, 0)
    ds_t = d_scores[...].T.astype(BF16)
    ds_low = d_scores[...].astype(BF16)
    db = dot_nn(ds_t, c_part)
    dc = dot_nn(ds_low, b_part)
    rows_each = T // NT
    for s in range(NT):
        b_out[s, :, :128] = db[s * rows_each : (s + 1) * rows_each]
        b_out[s, :, 128:] = dc[s * rows_each : (s + 1) * rows_each]

    def b_copy(k):
        to = (me + k) % NT
        return remote(b_out.at[to], b_in.at[k], bs_sem.at[k], br_sem.at[k], "tensor", to)

    loop(NT, lambda k: b_copy(k).start())

    lower = (iota((T, T), 0) >= iota((T, T), 1)).astype(F32)
    columns = col_sum[...]
    d_rate = jnp.dot(
        columns - row_sum[...], lower, precision=HIGH, preferred_element_type=F32
    )
    raw = dt_ref[...]
    step = softplus(raw)
    decay = head_rates(alog_ref)
    d_step = columns / step + decay * d_rate
    ddt_ref[...] = d_step / (1.0 + jnp.exp(-raw))
    pay[0:8, :] = stat_ref[...]
    pay[8:16, :] = jnp.broadcast_to(
        jnp.sum(d_rate * decay * step, axis=1, keepdims=True), (HEADS, BLK)
    )

    def pay_copy(k):
        return remote(pay, pay_in.at[k], ys_sem.at[k], yr_sem.at[k], "dp", (w + k) % NDP)

    loop(NDP, lambda k: pay_copy(k).start())

    def p_add(k, total):
        p_copy(k).wait_recv()
        return total + p_in[k]

    p_sum = lax.fori_loop(1, NDP, p_add, p_send[w]) / NDP
    p_own[...] = p_sum
    p_full[w] = p_sum

    def g_copy(k, slot):
        return remote(p_own, p_full.at[slot], gs_sem.at[k], gr_sem.at[k], "dp", (w + k) % NDP)

    loop(NDP, lambda k: g_copy(k, w).start())

    def b_add(k, total):
        b_copy(k).wait_recv()
        return total + b_in[k]

    b_total = lax.fori_loop(1, NT, b_add, b_out[me])
    b_sum[...] = b_total
    my_rows = pl.ds(pl.multiple_of(me * rows_each, 8), rows_each)
    dbc_ref[my_rows, :] = b_total

    def c_copy(k, slot):
        rows = pl.ds(pl.multiple_of(slot * rows_each, 8), rows_each)
        return remote(b_sum, dbc_ref.at[rows], cs_sem.at[k], cr_sem.at[k], "tensor", (me + k) % NT)

    loop(NT, lambda k: c_copy(k, me).start())

    loop(NDP, lambda k: g_copy(k, (w + NDP - k) % NDP).wait_recv())

    def gram_add(c, total):
        three = jnp.concatenate(split3(p_full[c]), axis=0)
        return total + dot_nt(three, three)

    g9 = lax.fori_loop(0, NDP, gram_add, jnp.zeros((3 * RANK, 3 * RANK), F32))
    g3 = g9[:RANK] + g9[RANK : 2 * RANK] + g9[2 * RANK :]
    gram = g3[:, :RANK] + g3[:, RANK : 2 * RANK] + g3[:, 2 * RANK :]
    eye = (iota((RANK, RANK), 0) == iota((RANK, RANK), 1)).astype(F32)
    table = jnp.concatenate([eye, gram], axis=1)
    places = iota((RANK, 2 * RANK), 0)
    for j in range(RANK - 1):
        column = table[:, RANK + j : RANK + j + 1]
        row = table[j : j + 1, :]
        pivot = table[j : j + 1, RANK + j : RANK + j + 1]
        table = table - jnp.where(places > j, column * (row / pivot), 0.0)
    pivots = jnp.sum(jnp.where(eye > 0.0, table[:, RANK:], 0.0), axis=1, keepdims=True)
    inverse = table[:, :RANK] * lax.rsqrt(pivots)

    for c in range(NDP):
        ph_ref[:, c * 256 : (c + 1) * 256] = jnp.dot(
            inverse, p_full[c], precision=HIGH, preferred_element_type=F32
        )

    e_load.wait()

    def q_part(s, carry):
        rotated, total = carry
        lanes = pl.ds(pl.multiple_of(s * CH, CH), CH)
        hi, lo = split2(ph_ref[:, lanes])
        two = jnp.concatenate([hi, lo], axis=0)
        rotated = rotated + dot_nt(two, xall[s])
        e_hi, e_lo = split2(e_all[lanes, :])
        both = dot_nn(two, e_hi)
        return rotated, total + both[:RANK] + both[RANK:] + dot_nn(hi, e_lo)

    rotated, total = lax.fori_loop(
        0, NT, q_part, (jnp.zeros((2 * RANK, T), F32), jnp.zeros((RANK, CH), F32))
    )
    two = jnp.concatenate(split2(rotated[:RANK] + rotated[RANK:]), axis=0)
    both = dot_nn(two, dxb)
    q_local = total + both[:RANK] + both[RANK:]
    for c in range(NDP):
        a, b = c // 4, c % 4
        q_out[c] = q_local[a * 8 : (a + 1) * 8, b * BLK : (b + 1) * BLK]

    def q_copy(k):
        to = (w + k) % NDP
        return remote(q_out.at[to], q_in.at[k], qs_sem.at[k], qr_sem.at[k], "dp", to)

    loop(NDP, lambda k: q_copy(k).start())

    def pay_add(k, total):
        pay_copy(k).wait_recv()
        return total + pay_in[k]

    pay_ref[...] = lax.fori_loop(1, NDP, pay_add, pay[...])

    def q_add(k, total):
        q_copy(k).wait_recv()
        return total + q_in[k]

    q_sum = lax.fori_loop(1, NDP, q_add, q_out[w]) / NDP
    q_own[...] = q_sum
    q_full[w] = q_sum

    def h_copy(k, slot):
        return remote(q_own, q_full.at[slot], hs_sem.at[k], hr_sem.at[k], "dp", (w + k) % NDP)

    loop(NDP, lambda k: h_copy(k, w).start())

    def d_add(k):
        d_copy(k).wait_recv()
        d_own[...] += d_in[k].astype(F32)

    loop(NT, d_add)
    dinp_ref[...] = d_own[...].astype(BF16)

    loop(NT, lambda k: c_copy(k, (me + NT - k) % NT).wait_recv())
    loop(NDP, lambda k: h_copy(k, (w + NDP - k) % NDP).wait_recv())
    for c in range(NDP):
        a, b = c // 4, c % 4
        qm_ref[a * 8 : (a + 1) * 8, b * BLK : (b + 1) * BLK] = q_full[c]

    def finish_workers(k):
        p_copy(k).wait_send()
        g_copy(k, w).wait_send()
        pay_copy(k).wait_send()
        q_copy(k).wait_send()
        h_copy(k, w).wait_send()

    def finish_shards(k):
        d_copy(k).wait_send()
        b_copy(k).wait_send()
        c_copy(k, me).wait_send()

    loop(NDP, finish_workers)
    loop(NT, finish_shards)


def error_kernel(
    e_ref, x_ref, dxb_ref, ph_ref, qm_ref, dinp_ref, dbc_ref, ddt_ref, dgate_ref,
    out_ref, ph_out, qm_out, dinp_out, dbc_out, ddt_out, dgate_out, right
):
    b = pl.program_id(0)

    @pl.when(b == 0)
    def _():
        q_hi, q_lo = split2(-qm_ref[...])
        right[:T] = dxb_ref[...]
        right[T : T + RANK] = q_hi
        right[T + RANK : T + 2 * RANK] = q_lo
        right[T + 2 * RANK :] = q_hi
        qm_out[...] = qm_ref[...]
        dinp_out[...] = dinp_ref[...]
        dbc_out[...] = dbc_ref[...]
        ddt_out[...] = ddt_ref[...]
        dgate_out[...] = dgate_ref[...]

    ph = ph_ref[...]
    ph_out[...] = ph
    hi, lo = split2(ph)
    left = jnp.concatenate([x_ref[0], hi, hi, lo], axis=0)
    out_ref[...] = e_ref[...] + lax.dot_general(
        left, right[...], (((0,), (0,)), ((), ())), preferred_element_type=F32
    )


def vmem():
    return pl.BlockSpec(memory_space=pltpu.VMEM)


def smem():
    return pl.BlockSpec(memory_space=pltpu.SMEM)


def hbm():
    return pl.BlockSpec(memory_space=pl.ANY)


def shape(dims, dtype=F32):
    return jax.ShapeDtypeStruct(dims, dtype)


DMA = pltpu.SemaphoreType.DMA


def shards(
    layer_input, w_x, gate_in, bc, dt_raw, a_log, skip, gain, doc_ids, d_out, q_prev, error_in
):
    doc_row = doc_ids.reshape(1, T)
    gain_row = gain.reshape(1, CH)
    xall, eq, inner, dxb, dy, d_gate, stat, cum, rowp = pl.pallas_call(
        forward_kernel,
        name="forward",
        out_shape=(
            shape((NT, T, CH), BF16), shape((RANK, D)), shape((T, CH), BF16), shape((T, CH), BF16),
            shape((T, CH), BF16), shape((T, CH), BF16), shape((8, BLK)), shape((HEADS, T)),
            shape((HEADS, T)),
        ),
        in_specs=[
            vmem(), hbm(), hbm(), vmem(), vmem(), vmem(), vmem(), smem(), smem(), vmem(), vmem(),
            vmem(),
        ],
        out_specs=(hbm(),) + (vmem(),) * 8,
        scratch_shapes=[
            pltpu.VMEM((NT, T, CH), BF16),
            pltpu.VMEM((D, CH), BF16),
            pltpu.VMEM((2, CH, CH), F32),
            pltpu.VMEM((HEADS, T, T), BF16),
            pltpu.VMEM((HEADS, T, T), BF16),
            pltpu.VMEM((8, BLK), F32),
            pltpu.VMEM((8, BLK), F32),
            pltpu.VMEM((T, T), F32),
            pltpu.VMEM((T, T), F32),
            pltpu.VMEM((T, T), F32),
            pltpu.VMEM((T, T), F32),
            pltpu.VMEM((T, CH), F32),
            pltpu.VMEM((T, CH), F32),
            pltpu.VMEM((8, T), F32),
            pltpu.VMEM((NT, 8, T), F32),
            DMA((3, NT, 2)),
            DMA((NT, 2)),
            DMA((NT,)),
            DMA((NT,)),
            DMA((NT,)),
            DMA((2,)),
            DMA,
        ],
        compiler_params=pltpu.CompilerParams(
            collective_id=0, has_side_effects=True, vmem_limit_bytes=VMEM_LIMIT
        ),
    )(
        layer_input, w_x, error_in, gate_in, d_out, bc, dt_raw, a_log, skip, gain_row, doc_row,
        q_prev,
    )
    ph, qm, d_input, d_bc, d_dt, pay = pl.pallas_call(
        factor_kernel,
        name="factor",
        out_shape=(
            shape((RANK, D)), shape((RANK, CH)), shape((T, CH), BF16), shape((T, 256)),
            shape((HEADS, T)), shape((16, BLK)),
        ),
        in_specs=[hbm()] * 3 + [vmem()] * 10 + [smem(), vmem()],
        out_specs=(vmem(),) * 6,
        scratch_shapes=[
            pltpu.VMEM((NT, T, CH), BF16),
            pltpu.VMEM((D, CH), F32),
            pltpu.VMEM((D, CH), BF16),
            pltpu.VMEM((NDP, RANK, 256), F32),
            pltpu.VMEM((NDP, RANK, 256), F32),
            pltpu.VMEM((RANK, 256), F32),
            pltpu.VMEM((NDP, RANK, 256), F32),
            pltpu.VMEM((NT, T, CH), BF16),
            pltpu.VMEM((NT, T, CH), BF16),
            pltpu.VMEM((T, CH), F32),
            pltpu.VMEM((NT, T // NT, 256), F32),
            pltpu.VMEM((NT, T // NT, 256), F32),
            pltpu.VMEM((T // NT, 256), F32),
            pltpu.VMEM((T, T), F32),
            pltpu.VMEM((T, T), F32),
            pltpu.VMEM((T, T), F32),
            pltpu.VMEM((HEADS, T), F32),
            pltpu.VMEM((HEADS, T), F32),
            pltpu.VMEM((16, BLK), F32),
            pltpu.VMEM((NDP, 16, BLK), F32),
            pltpu.VMEM((NDP, 8, BLK), F32),
            pltpu.VMEM((NDP, 8, BLK), F32),
            pltpu.VMEM((8, BLK), F32),
            pltpu.VMEM((NDP, 8, BLK), F32),
            DMA((2,)),
            DMA,
            DMA((NDP,)), DMA((NDP,)), DMA((NDP,)), DMA((NDP,)),
            DMA((NT,)), DMA((NT,)), DMA((NT,)), DMA((NT,)), DMA((NT,)), DMA((NT,)),
            DMA((NDP,)), DMA((NDP,)), DMA((NDP,)), DMA((NDP,)), DMA((NDP,)), DMA((NDP,)),
        ],
        compiler_params=pltpu.CompilerParams(
            collective_id=1, has_side_effects=True, vmem_limit_bytes=VMEM_LIMIT
        ),
    )(
        xall, error_in, w_x, eq, dxb, dy, inner, q_prev, bc, cum, rowp, dt_raw, doc_row, a_log,
        stat,
    )

    def whole(dims):
        return pl.BlockSpec(dims, lambda b: (0,) * len(dims))

    error_out, p_factor, right_mean, d_input, d_bc, d_dt, d_gate = pl.pallas_call(
        error_kernel,
        name="error",
        grid=(NT,),
        out_shape=(
            shape((D, CH)), shape((RANK, D)), shape((RANK, CH)), shape((T, CH), BF16),
            shape((T, 256)), shape((HEADS, T)), shape((T, CH), BF16),
        ),
        in_specs=[
            pl.BlockSpec((CH, CH), lambda b: (b, 0)),
            pl.BlockSpec((1, T, CH), lambda b: (b, 0, 0)),
            whole((T, CH)),
            pl.BlockSpec((RANK, CH), lambda b: (0, b)),
            whole((RANK, CH)),
            whole((T, CH)),
            whole((T, 256)),
            whole((HEADS, T)),
            whole((T, CH)),
        ],
        out_specs=(
            pl.BlockSpec((CH, CH), lambda b: (b, 0)),
            pl.BlockSpec((RANK, CH), lambda b: (0, b)),
            whole((RANK, CH)),
            whole((T, CH)),
            whole((T, 256)),
            whole((HEADS, T)),
            whole((T, CH)),
        ),
        scratch_shapes=[pltpu.VMEM((T + 3 * RANK, CH), BF16)],
        compiler_params=pltpu.CompilerParams(vmem_limit_bytes=VMEM_LIMIT),
    )(error_in, xall, dxb, ph, qm, d_input, d_bc, d_dt, d_gate)
    d_gain = pay[0:4].reshape(CH)
    d_skip = jnp.sum(pay[4:8].reshape(HEADS, 64), axis=1)
    d_alog = pay[8:16, 0]
    return (
        d_input, d_gate, d_bc, d_dt, d_alog, d_skip, d_gain, p_factor, right_mean, error_out,
    )


def solution(mesh):
    return jax.shard_map(
        shards,
        mesh=mesh,
        in_specs=(
            P("dp", "tensor"),
            P(None, "tensor"),
            P("dp", "tensor"),
            P("dp", None),
            P("tensor", "dp"),
            P("tensor"),
            P("tensor"),
            P("tensor"),
            P("dp"),
            P("dp", "tensor"),
            P(None, "tensor"),
            P("dp", "tensor"),
        ),
        out_specs=(
            P("dp", "tensor"),
            P("dp", "tensor"),
            P("dp", None),
            P("tensor", "dp"),
            P("tensor"),
            P("tensor"),
            P("tensor"),
            P("tensor", None),
            P(None, "tensor"),
            P("dp", "tensor"),
        ),
        check_vma=False,
    )
```

time: 879 us -> 143 us (0.16)
  waiting for transfers between devices: 476 us -> 0 us
  matrix products: 164 us -> 0 us
  Pallas kernels: 0 us -> 137 us
  local copies, waits for them, and re-layouts: 79 us -> 3.96 us
  blocking collectives: 60.7 us -> 0 us
  loops' own time: 40.3 us -> 0 us
  other arithmetic: 39.2 us -> 0.63 us
  between operations: 14 us -> 0.66 us
    psum x3 -> x0, waiting for transfers between devices: 300 us -> none  [the longest x1 145 us: shards(): factor_sum = lax.psum(factor, 'dp')]
    dot_general x161 -> x0, matrix products: 164 us -> none  [the longest x64 43.4 us: add_column(): column = column - jnp.dot(basis, coefficients, precision=HIGH)]
    pallas_call x0 -> x3, Pallas kernels: none -> 137 us  [the longest x1 85.8 us: shards(): pl.pallas_call(factor_kernel, name='factor', out_shape=(shape((RANK, D)),...]
    reduce_scatter x1 -> x0, waiting for transfers between devices: 111 us -> none  [shards(): lax.psum_scatter(lax.dot_general(w_x, grad_inner, (((1,), (1,)), ((), ())...]
    all_gather x1 -> x0, waiting for transfers between devices: 64.5 us -> none  [shards(): token_rows = lax.all_gather(layer_input, 'tensor', axis=1, tiled=True)]
    psum x3 -> x0, blocking collectives: 60.7 us -> none  [the longest x1 34 us: shards(): lax.psum((gain_part, grad_decay, grad_skip), 'dp')]
    another operation x3 -> x0, loops' own time: 40.3 us -> none  [the longest x1 23.4 us: gram_orthonormal(): basis = lax.fori_loop(0, rank_count, add_column, jnp.zeros_like(factor))]
    unnamed x28 -> x0, local copies, waits for them, and re-layouts: 26.5 us -> none
  transfers between devices with their start and end apart: 5 -> 0, of which waited for: 5 -> 0; matrix products, arithmetic and copies ran while one was open for 5% -> 0% of each run, Pallas kernels for 0% -> 0%
where the time goes in v1:
time: 143 us; the launch traced here: 142 us
  Pallas kernels  137 us (96%)
  local copies, waits for them, and re-layouts  3.96 us (3%)
    pallas_call x1, Pallas kernels, shards(): pl.pallas_call(factor_kernel, name='factor', out_shape=(shape((RANK, D)),...  85.8 us
    pallas_call x1, Pallas kernels, shards(): pl.pallas_call(forward_kernel, name='forward', out_shape=(shape((NT, T, C...  39.1 us
    pallas_call x1, Pallas kernels, shards(): pl.pallas_call(error_kernel, name='error', grid=(NT,), out_shape=(shape((...  12.1 us

profile of v1, /device:TPU:1, one launch (start us, length us, event | category | flops | bytes accessed | tf_op | source)
XLA Modules:
  0.0 142.2 jit_solution(7391107256739681531)
XLA Ops:
  0.6 1.2 reshape.33.doc_ref
  1.9 39.1 %forward.1 = (bf16[8,384,512]{2,1,0:T(8,128)(2,1)}, f32[32,4096]{1,0:T(8,128)}, bf16[384,512]{1,0:T(8,128)(2,1)}, bf16[384,512]{1,0:T(8,128)(2,1)}, bf16[384,512...) custom-call(bf16[384,512]{1,0:T(8,128)(2,1)} %x_ref.1, ...), custom_call_target="tpu_custom_call" | custom-call | tf_op jit(solution)/shard_map/forward/pallas_call | solution.py:653
  41.0 85.8 %factor.1 = (f32[32,4096]{1,0:T(8,128)}, f32[32,512]{1,0:T(8,128)}, bf16[384,512]{1,0:T(8,128)(2,1)}, f32[384,256]{1,0:T(8,128)}, f32[8,384]{1,0:T(8,128)}, /*index=5*/f32[16,128]{1,0:T(8,128)}) custom-call(bf16[8,384,512]{2,1,0:T(8,128)(2,1)} %get-tuple-element.32.xall_hbm.x_ref, f32[4096,512]{1,0:T(8,128)} %e_ref.1, bf16[4096,512]{1,0:T(8,128)(2,1)} %wx_hbm.3, ...), custom_call_target="tpu_custom_call" | custom-call | tf_op jit(solution)/shard_map/factor/pallas_call | solution.py:697
  126.7 1.3 slice_reduce_fusion
  128.0 1.3 slice_bitcast_fusion
  129.4 0.1 reshape.34
  129.4 0.6 reduce_sum.9
  130.1 12.1 %error.1 = (f32[4096,512]{1,0:T(8,128)}, f32[32,4096]{1,0:T(8,128)}, f32[32,512]{1,0:T(8,128)}, bf16[384,512]{1,0:T(8,128)(2,1)}, f32[384,256]{1,0:T(8,128)}, /*...) custom-call(f32[4096,512]{1,0:T(8,128)} %e_ref.1, bf16[8,384,512]{2,1,0:T(8,128)(2,1)} %get-tuple-element.32.xall_hbm.x_ref, ...), custom_call_target="tpu_custom_call" | custom-call | tf_op jit(solution)/shard_map/error/pallas_call | solution.py:748

commit v2 on v1

v2 whole, which is shorter than its diff:
```python
import jax
import jax.numpy as jnp
from jax import lax
from jax.experimental import pallas as pl
from jax.experimental.pallas import tpu as pltpu
from jax.sharding import PartitionSpec as P

EPSILON = 1e-05
HIGH = lax.Precision.HIGHEST
MESH = pl.DeviceIdType.MESH
F32 = jnp.float32
BF16 = jnp.bfloat16
T = 384
HALF = T // 2
HEADS = 8
CH = 512
NT = 8
NDP = 16
D = 4096
RANK = 32
BLK = 128
NB = T // BLK
LOW = -1e30
VMEM_LIMIT = 56 * 1024 * 1024


def dot_nn(a, b):
    return lax.dot_general(a, b, (((1,), (0,)), ((), ())), preferred_element_type=F32)


def dot_nt(a, b):
    return lax.dot_general(a, b, (((1,), (1,)), ((), ())), preferred_element_type=F32)


def split2(v):
    hi = v.astype(BF16)
    lo = (v - hi.astype(F32)).astype(BF16)
    return hi, lo


def split3(v):
    hi = v.astype(BF16)
    rest = v - hi.astype(F32)
    mid = rest.astype(BF16)
    lo = (rest - mid.astype(F32)).astype(BF16)
    return hi, mid, lo


def iota(shape, dim):
    return lax.broadcasted_iota(jnp.int32, shape, dim)


def to_column(row):
    return jnp.broadcast_to(row, (BLK, row.shape[1])).T


def head_rates(alog_ref):
    rows = iota((HEADS, T), 0)
    logs = jnp.zeros((HEADS, T), F32)
    for h in range(HEADS):
        logs = jnp.where(rows == h, alog_ref[h], logs)
    return jnp.exp(logs)


def softplus(v):
    return jnp.maximum(v, 0.0) + jnp.log1p(jnp.exp(-jnp.abs(v)))


def keep_bias(doc_ref, bias_ref, bias_t_ref):
    doc_row = doc_ref[...].astype(F32).reshape(1, T)
    doc_col = to_column(doc_row)
    for i in range(NB):
        for j in range(NB):
            rows = iota((BLK, BLK), 0) + i * BLK
            cols = iota((BLK, BLK), 1) + j * BLK
            same = doc_col[i * BLK : (i + 1) * BLK] == doc_row[:, j * BLK : (j + 1) * BLK]
            spot = (slice(i * BLK, (i + 1) * BLK), slice(j * BLK, (j + 1) * BLK))
            bias_ref[spot] = jnp.where(jnp.logical_and(same, rows >= cols), 0.0, LOW)
            if bias_t_ref is not None:
                bias_t_ref[spot] = jnp.where(jnp.logical_and(same, rows <= cols), 0.0, LOW)


def main_kernel(
    x_ref, wx_hbm, e_hbm, gate_ref, dout_ref, bc_ref, dt_ref, alog_ref, skip_ref, gain_ref,
    doc_ref, q_ref,
    m_hbm, ph_ref, qm_ref, dinp_ref, dbc_ref, ddt_ref, dgate_ref, pay_ref,
    xall, wx, e_all, eq_ref, w_mat, wt_mat, bias, bias_t, scores, scores_t, d_scores,
    cum_ref, rowp_ref, row_sum, col_sum, acc, y_buf, inner_ref, dxb_ref, dy_ref, sums, sums_in,
    p_send, core_in, p_mid, y_in, p_low, x_in, p_full,
    dx_out, part_out, opp_out, near_out, near_hold, dx_in, part_in, opp_in, near_in,
    bc_part, b_out, b_in, b_full, pay, pay_in, q_out, q_in, q_own, q_full,
    x_send, x_recv, s_send, s_recv, wx_sem, e_sem, m_sem,
    core_sem, y_send, y_recv, low_sem, g_send, g_recv,
    dx_send, dx_recv, part_send, part_recv, opp_send, opp_recv, near_send, near_recv,
    bs_sem, br_sem, cs_sem, cr_sem,
    ys_sem, yr_sem, qs_sem, qr_sem, hs_sem, hr_sem,
):
    me = lax.axis_index("tensor")
    z = me // 2
    xl = me % 2
    zp = ((z + 1) % 4) * 2 + xl
    zm = ((z + 3) % 4) * 2 + xl
    zo = ((z + 2) % 4) * 2 + xl
    xp = z * 2 + (1 - xl)

    w = lax.axis_index("dp")
    core = w % 2
    xh = (w // 2) % 2
    y = w // 4
    other_core = w + 1 - 2 * core
    other_x = w + 2 - 4 * xh

    def y_peer(k):
        return ((y + k) % 4) * 4 + xh * 2 + core

    def loop(count, step_body):
        def step(k, carry):
            step_body(k)
            return carry

        lax.fori_loop(1, count, step, 0)

    barrier = pltpu.get_barrier_semaphore()

    def greet(axis, to):
        pl.semaphore_signal(barrier, inc=1, device_id={axis: to}, device_id_type=MESH)

    loop(NT, lambda k: greet("tensor", (me + k) % NT))
    loop(NDP, lambda k: greet("dp", (w + k) % NDP))

    def wx_copy(b):
        rows = pl.ds(b * CH, CH)
        return pltpu.make_async_copy(wx_hbm.at[rows], wx.at[rows], wx_sem.at[b])

    def e_copy(b):
        rows = pl.ds(b * CH, CH)
        return pltpu.make_async_copy(e_hbm.at[rows], e_all.at[rows], e_sem.at[b])

    for b in range(NT):
        e_copy(b).start()
    for b in range(NT):
        wx_copy(b).start()

    xall[me] = x_ref[...]
    pl.semaphore_wait(barrier, NT - 1 + NDP - 1)

    def x_copy(way, to, src, half):
        part = xall.at[src, pl.ds(half * HALF, HALF)]
        return pltpu.make_async_remote_copy(
            src_ref=part,
            dst_ref=part,
            send_sem=x_send.at[way, src, half],
            recv_sem=x_recv.at[src, half],
            device_id={"tensor": to},
            device_id_type=MESH,
        )

    sent = []

    def send(way, to, src, half):
        copy = x_copy(way, to, src, half)
        copy.start()
        sent.append(copy)

    def arrive(src, half):
        x_copy(0, zp, src, half).wait_recv()

    for half in range(2):
        send(0, zp, me, half)
        send(1, zm, me, half)
        send(2, xp, me, half)

    step = softplus(dt_ref[...])
    rate = head_rates(alog_ref) * step
    upper = (iota((T, T), 0) <= iota((T, T), 1)).astype(F32)
    cum = jnp.dot(rate, upper, precision=HIGH, preferred_element_type=F32)
    cum_ref[...] = cum
    rowp_ref[...] = cum + jnp.log(step)
    keep_bias(doc_ref, bias, bias_t)
    b_part = bc_ref[:, :128]
    c_part = bc_ref[:, 128:]
    scores[...] = dot_nt(c_part, b_part)
    scores_t[...] = dot_nt(b_part, c_part)

    q_hi, q_lo = split2(q_ref[...])
    q_two = jnp.concatenate([q_hi, q_lo], axis=0)

    def e_block(b):
        e_copy(b).wait()
        e_hi, e_lo = split2(e_all[b * CH : (b + 1) * CH])
        both = dot_nt(q_two, e_hi)
        eq_ref[:, b * CH : (b + 1) * CH] = both[:RANK] + both[RANK:] + dot_nt(q_hi, e_lo)

    for b in range(NT):
        e_block(b)

    arrive(zm, 0)
    send(0, zp, zm, 0)
    arrive(xp, 0)
    send(0, zp, xp, 0)
    send(1, zm, xp, 0)

    def weights(h, carry):
        cum_row = cum_ref[pl.ds(h, 1), :]
        rowp_row = rowp_ref[pl.ds(h, 1), :]
        col = to_column(cum_row)
        colp = to_column(rowp_row)
        for i in range(NB):
            here = slice(i * BLK, (i + 1) * BLK)
            for j in range(NB):
                there = slice(j * BLK, (j + 1) * BLK)
                if j <= i:
                    span = rowp_row[:, there] - col[here] + bias[here, there]
                    w_mat[h, here, there] = (scores[here, there] * jnp.exp(span)).astype(BF16)
                if j >= i:
                    span = colp[here] - cum_row[:, there] + bias_t[here, there]
                    wt_mat[h, here, there] = (scores_t[here, there] * jnp.exp(span)).astype(BF16)
        return carry

    lax.fori_loop(0, HEADS, weights, 0)

    arrive(zp, 1)
    send(1, zm, zp, 1)
    arrive(xp, 1)
    send(0, zp, xp, 1)
    send(1, zm, xp, 1)

    for b in range(NT):
        wx_copy(b).wait()
    arrive(zm, 1)
    arrive(zp, 0)

    def product(src):
        rows = pl.ds(pl.multiple_of(src * CH, CH), CH)
        return dot_nn(xall[src], wx[rows, :])

    acc[...] = product(me) + product(xp)
    acc[...] += product(zm) + product(zp)
    arrive(zo, 0)
    send(2, xp, zo, 0)
    arrive(zo, 1)
    send(2, xp, zo, 1)
    acc[...] += product(zo)
    xp_zp = ((z + 1) % 4) * 2 + (1 - xl)
    xp_zm = ((z + 3) % 4) * 2 + (1 - xl)
    xp_zo = ((z + 2) % 4) * 2 + (1 - xl)
    for other in (xp_zp, xp_zm, xp_zo):
        arrive(other, 0)
        arrive(other, 1)
        acc[...] += product(other)
    inner_ref[...] = acc[...].astype(BF16)

    low_lanes = iota((1, BLK), 1) < 64

    def pair_lanes(p):
        return pl.ds(pl.multiple_of(p * BLK, BLK), BLK)

    def pair_skip(p):
        return jnp.where(low_lanes, skip_ref[2 * p], skip_ref[2 * p + 1])

    def gate_parts(lanes):
        gate = gate_ref[:, lanes].astype(F32)
        sig = 1.0 / (1.0 + jnp.exp(-gate))
        return gate, sig, gate * sig

    def mix(p, carry):
        square, product_sum = carry
        lanes = pair_lanes(p)
        x_pair = inner_ref[:, lanes]
        for i in range(NB):
            here = slice(i * BLK, (i + 1) * BLK)
            width = (i + 1) * BLK
            first = dot_nn(w_mat[2 * p, here, :width], x_pair[:width])
            second = dot_nn(w_mat[2 * p + 1, here, :width], x_pair[:width])
            y_buf[here, lanes] = jnp.where(low_lanes, first, second) + pair_skip(
                p
            ) * x_pair[here].astype(F32)
        gate, sig, silu = gate_parts(lanes)
        g = y_buf[:, lanes] * silu
        weighted = dout_ref[:, lanes].astype(F32) * gain_ref[lanes].reshape(1, BLK)
        return square + g * g, product_sum + g * weighted

    zero = jnp.zeros((T, BLK), F32)
    square, product_sum = lax.fori_loop(0, HEADS // 2, mix, (zero, zero))
    sums[0:1, :] = jnp.sum(square.T, axis=0, keepdims=True)
    sums[1:2, :] = jnp.sum(product_sum.T, axis=0, keepdims=True)
    sums[2:8, :] = jnp.zeros((6, T), F32)

    def s_copy(k):
        return pltpu.make_async_remote_copy(
            src_ref=sums,
            dst_ref=sums_in.at[k],
            send_sem=s_send.at[k],
            recv_sem=s_recv.at[k],
            device_id={"tensor": (me + k) % NT},
            device_id_type=MESH,
        )

    for k in range(1, NT):
        s_copy(k).start()
    total = sums[...]
    for k in range(1, NT):
        s_copy(k).wait_recv()
        total = total + sums_in[k]
    r_row = lax.rsqrt(total[0:1] / D + EPSILON)
    r_col = to_column(r_row)
    m_col = to_column(r_row * r_row * r_row * (total[1:2] / D))

    def back(p, carry):
        lanes = pair_lanes(p)
        gate, sig, silu = gate_parts(lanes)
        mixed = y_buf[:, lanes]
        g = mixed * silu
        up = dout_ref[:, lanes].astype(F32)
        dg = r_col * (up * gain_ref[lanes].reshape(1, BLK)) - g * m_col
        dgate_ref[:, lanes] = (dg * mixed * sig * (1.0 + gate * (1.0 - sig))).astype(BF16)
        dy = dg * silu
        dy_low = dy.astype(BF16)
        dy_ref[:, lanes] = dy_low
        pay[pl.ds(p, 1), :] = jnp.sum(up * g * r_col, axis=0, keepdims=True)
        pay[pl.ds(4 + p, 1), :] = jnp.sum(
            dy * inner_ref[:, lanes].astype(F32), axis=0, keepdims=True
        )
        for i in range(NB):
            here = slice(i * BLK, (i + 1) * BLK)
            first = dot_nn(wt_mat[2 * p, here, i * BLK :], dy_low[i * BLK :])
            second = dot_nn(wt_mat[2 * p + 1, here, i * BLK :], dy_low[i * BLK :])
            dxb_ref[here, lanes] = (
                jnp.where(low_lanes, first, second) + pair_skip(p) * dy[here]
            ).astype(BF16)
        return carry

    lax.fori_loop(0, HEADS // 2, back, 0)


    def remote(src, dst, send_sem, recv_sem, axis, to):
        copy = pltpu.make_async_remote_copy(
            src_ref=src, dst_ref=dst, send_sem=send_sem, recv_sem=recv_sem,
            device_id={axis: to}, device_id_type=MESH,
        )
        return copy

    def begin(copy):
        copy.start()
        sent.append(copy)

    dxb = dxb_ref[...]
    q3 = jnp.concatenate(split3(q_ref[...]), axis=0)
    z3 = dot_nt(q3, dxb)
    z_sum = z3[:RANK] + z3[RANK : 2 * RANK] + z3[2 * RANK :]
    z_three = jnp.concatenate(split3(z_sum), axis=0)
    for s in range(NT):
        part = dot_nn(z_three, xall[s])
        part = part[:RANK] + part[RANK : 2 * RANK] + part[2 * RANK :]
        part = part + eq_ref[:, s * CH : (s + 1) * CH]
        p_send[2 * s] = part[:, :256]
        p_send[2 * s + 1] = part[:, 256:]
    core_copy = remote(
        p_send.at[pl.ds((1 - core) * 8, 8)], core_in, core_sem.at[0], core_sem.at[1], "dp",
        other_core,
    )
    begin(core_copy)

    def input_part(s):
        rows = pl.ds(pl.multiple_of(s * CH, CH), CH)
        return dot_nt(dxb, wx[rows, :])

    def dx_copy(i):
        return remote(dx_out.at[i], dx_in.at[i], dx_send.at[i], dx_recv.at[i], "tensor", xp)

    ways = (zp, zm)

    def part_copy(i):
        return remote(
            part_out.at[i], part_in.at[i], part_send.at[i], part_recv.at[i], "tensor", ways[i]
        )

    def opp_copy(i):
        return remote(
            opp_out.at[i], opp_in.at[i], opp_send.at[i], opp_recv.at[i], "tensor", ways[i]
        )

    def near_copy(i, half):
        return remote(
            near_out.at[i, pl.ds(half * HALF, HALF)], near_in.at[i, half],
            near_send.at[i, half], near_recv.at[i, half], "tensor", ways[i],
        )

    dx_out[0] = input_part(xp_zo).astype(BF16)
    begin(dx_copy(0))
    part_out[0] = input_part(xp_zp).astype(BF16)
    begin(part_copy(0))
    part_out[1] = input_part(xp_zm).astype(BF16)
    begin(part_copy(1))

    core_copy.wait_recv()
    for c in range(8):
        p_mid[c] = p_send[core * 8 + c] + core_in[c]

    def y_copy(k):
        to = y_peer(k)
        return remote(
            p_mid.at[pl.ds((to // 4) * 2, 2)], y_in.at[k], y_send.at[k], y_recv.at[k], "dp", to
        )

    for k in range(1, 4):
        begin(y_copy(k))

    to_zp = input_part(zp)
    near_out[0, HALF:] = to_zp[HALF:].astype(BF16)
    near_hold[0] = to_zp[:HALF]
    begin(near_copy(0, 1))
    to_zm = input_part(zm)
    near_out[1, :HALF] = to_zm[:HALF].astype(BF16)
    near_hold[1] = to_zm[HALF:]
    begin(near_copy(1, 0))

    d_scores[...] = jnp.zeros((T, T), F32)

    def head_back(p):
        lanes = slice(p * BLK, (p + 1) * BLK)
        x_pair = inner_ref[:, lanes]
        dy_pair = dy_ref[:, lanes]
        for side in range(2):
            h = 2 * p + side
            mine = low_lanes if side == 0 else jnp.logical_not(low_lanes)
            x_mine = jnp.where(mine, x_pair, jnp.zeros_like(x_pair))
            rowp_row = rowp_ref[h : h + 1, :]
            col = to_column(cum_ref[h : h + 1, :])
            downs = [jnp.zeros((1, BLK), F32) for _ in range(NB)]
            for i in range(NB):
                here = slice(i * BLK, (i + 1) * BLK)
                d_weight = dot_nt(dy_pair[here], x_mine[: (i + 1) * BLK])
                across = jnp.zeros((BLK, BLK), F32)
                for j in range(i + 1):
                    there = slice(j * BLK, (j + 1) * BLK)
                    span = rowp_row[:, there] - col[here] + bias[here, there]
                    d_score = d_weight[:, there] * jnp.exp(span)
                    d_scores[here, there] += d_score
                    both = d_score * scores[here, there]
                    downs[j] = downs[j] + jnp.sum(both, axis=0, keepdims=True)
                    across = across + both
                row_sum[h : h + 1, here] = jnp.sum(across.T, axis=0, keepdims=True)
            for j in range(NB):
                col_sum[h : h + 1, j * BLK : (j + 1) * BLK] = downs[j]

    def m_copy(s):
        rows = pl.ds(s * CH, CH)
        return pltpu.make_async_copy(e_all.at[rows], m_hbm.at[rows], m_sem.at[s])

    def merge(s):
        rows = slice(s * CH, (s + 1) * CH)
        e_all[rows] += lax.dot_general(
            xall[s], dxb_ref[...], (((0,), (0,)), ((), ())), preferred_element_type=F32
        )
        m_copy(s).start()

    head_back(0)
    merge(0)
    for k in range(1, 4):
        y_copy(k).wait_recv()
    for c in range(2):
        p_low[c] = p_mid[y * 2 + c] + y_in[1, c] + y_in[2, c] + y_in[3, c]
    low_copy = remote(p_low.at[1 - xh], x_in, low_sem.at[0], low_sem.at[1], "dp", other_x)
    begin(low_copy)

    head_back(1)
    merge(1)
    low_copy.wait_recv()
    mine = core * 8 + y * 2 + xh
    p_full[mine] = (p_low[xh] + x_in[...]) / NDP

    def g_copy(chunk, to, n):
        return remote(
            p_full.at[chunk], p_full.at[chunk], g_send.at[n], g_recv.at[chunk], "dp", to
        )

    begin(g_copy(mine, other_x, 0))
    for k in range(1, 4):
        begin(g_copy(mine, y_peer(k), k))
    begin(g_copy(mine, other_core, 4))

    dx_copy(0).wait_recv()
    opposite = input_part(zo) + dx_in[0].astype(F32)
    for i in range(2):
        opp_out[i] = opposite[i * HALF : (i + 1) * HALF].astype(BF16)
        begin(opp_copy(i))

    across_x = core * 8 + y * 2 + 1 - xh
    g_copy(across_x, other_x, 0).wait_recv()
    for k in range(1, 4):
        begin(g_copy(across_x, y_peer(k), 4 + k))
    begin(g_copy(across_x, other_core, 8))

    part_copy(0).wait_recv()
    part_copy(1).wait_recv()
    dx_out[1] = (
        input_part(xp) + part_in[0].astype(F32) + part_in[1].astype(F32)
    ).astype(BF16)
    begin(dx_copy(1))

    for k in range(1, 4):
        for c in range(2):
            chunk = core * 8 + ((y + k) % 4) * 2 + c
            g_copy(chunk, other_core, 0).wait_recv()
            begin(g_copy(chunk, other_core, 7 + 2 * k + c))

    head_back(2)
    head_back(3)
    for s in range(2, NT):
        merge(s)

    for i in range(2):
        half = i
        rows = slice(half * HALF, (half + 1) * HALF)
        opp_copy(i).wait_recv()
        near_out[i, rows] = (near_hold[i] + opp_in[i].astype(F32)).astype(BF16)
        begin(near_copy(i, half))

    for c in range(8):
        chunk = (1 - core) * 8 + c
        g_copy(chunk, other_core, 0).wait_recv()

    def gram_add(c, total):
        three = jnp.concatenate(split3(p_full[c]), axis=0)
        return total + dot_nt(three, three)

    g9 = lax.fori_loop(0, NDP, gram_add, jnp.zeros((3 * RANK, 3 * RANK), F32))
    g3 = g9[:RANK] + g9[RANK : 2 * RANK] + g9[2 * RANK :]
    gram = g3[:, :RANK] + g3[:, RANK : 2 * RANK] + g3[:, 2 * RANK :]
    eye = (iota((RANK, RANK), 0) == iota((RANK, RANK), 1)).astype(F32)
    table = jnp.concatenate([eye, gram], axis=1)
    places = iota((RANK, 2 * RANK), 0)
    for j in range(RANK - 1):
        column = table[:, RANK + j : RANK + j + 1]
        row = table[j : j + 1, :]
        pivot = table[j : j + 1, RANK + j : RANK + j + 1]
        table = table - jnp.where(places > j, column * (row / pivot), 0.0)
    pivots = jnp.sum(jnp.where(eye > 0.0, table[:, RANK:], 0.0), axis=1, keepdims=True)
    inverse = table[:, :RANK] * lax.rsqrt(pivots)

    for c in range(NDP):
        ph_ref[:, c * 256 : (c + 1) * 256] = jnp.dot(
            inverse, p_full[c], precision=HIGH, preferred_element_type=F32
        )

    def q_part(s, total):
        lanes = pl.ds(pl.multiple_of(s * CH, CH), CH)
        hi, lo = split2(ph_ref[:, lanes])
        two = jnp.concatenate([hi, lo], axis=0)
        m_hi, m_lo = split2(e_all[lanes, :])
        both = dot_nn(two, m_hi)
        return total + both[:RANK] + both[RANK:] + dot_nn(hi, m_lo)

    q_local = lax.fori_loop(0, NT, q_part, jnp.zeros((RANK, CH), F32))
    for c in range(NDP):
        a, b = c // 4, c % 4
        q_out[c] = q_local[a * 8 : (a + 1) * 8, b * BLK : (b + 1) * BLK]

    def q_copy(k):
        to = (w + k) % NDP
        return remote(q_out.at[to], q_in.at[k], qs_sem.at[k], qr_sem.at[k], "dp", to)

    loop(NDP, lambda k: q_copy(k).start())

    bc_part[:, :128] = dot_nn(d_scores[...].T.astype(BF16), c_part)
    bc_part[:, 128:] = dot_nn(d_scores[...].astype(BF16), b_part)
    rows_each = T // NT
    for s in range(NT):
        b_out[s] = bc_part[s * rows_each : (s + 1) * rows_each].astype(BF16)

    def b_copy(k):
        to = (me + k) % NT
        return remote(b_out.at[to], b_in.at[k], bs_sem.at[k], br_sem.at[k], "tensor", to)

    loop(NT, lambda k: b_copy(k).start())

    lower = (iota((T, T), 0) >= iota((T, T), 1)).astype(F32)
    columns = col_sum[...]
    d_rate = jnp.dot(columns - row_sum[...], lower, precision=HIGH, preferred_element_type=F32)
    raw = dt_ref[...]
    step = softplus(raw)
    decay = head_rates(alog_ref)
    d_step = columns / step + decay * d_rate
    ddt_ref[...] = d_step / (1.0 + jnp.exp(-raw))
    pay[8:16, :] = jnp.broadcast_to(
        jnp.sum(d_rate * decay * step, axis=1, keepdims=True), (HEADS, BLK)
    )
    pay_in[w] = pay[...]

    def pay_copy(k, slot):
        return remote(pay, pay_in.at[slot], ys_sem.at[k], yr_sem.at[k], "dp", (w + k) % NDP)

    loop(NDP, lambda k: pay_copy(k, w).start())

    def q_add(k, total):
        q_copy(k).wait_recv()
        return total + q_in[k]

    q_sum = lax.fori_loop(1, NDP, q_add, q_out[w]) / NDP
    q_own[...] = q_sum
    q_full[w] = q_sum

    def h_copy(k, slot):
        return remote(q_own, q_full.at[slot], hs_sem.at[k], hr_sem.at[k], "dp", (w + k) % NDP)

    loop(NDP, lambda k: h_copy(k, w).start())

    def b_add(k, total):
        b_copy(k).wait_recv()
        return total + b_in[k].astype(F32)

    my_rows = pl.ds(pl.multiple_of(me * rows_each, 16), rows_each)
    b_full[me] = lax.fori_loop(1, NT, b_add, bc_part[my_rows, :]).astype(BF16)

    def c_copy(k, slot):
        return remote(
            b_full.at[slot], b_full.at[slot], cs_sem.at[k], cr_sem.at[k], "tensor", (me + k) % NT
        )

    loop(NT, lambda k: c_copy(k, me).start())

    total = input_part(me)
    for i in range(2):
        for half in range(2):
            near_copy(i, half).wait_recv()
    dx_copy(1).wait_recv()
    for half in range(2):
        rows = slice(half * HALF, (half + 1) * HALF)
        dinp_ref[rows] = (
            total[rows] + near_in[0, half].astype(F32) + near_in[1, half].astype(F32)
            + dx_in[1, rows].astype(F32)
        ).astype(BF16)

    loop(NDP, lambda k: pay_copy(k, (w + NDP - k) % NDP).wait_recv())
    pay_ref[...] = lax.fori_loop(1, NDP, lambda c, t: t + pay_in[c], pay_in[0])
    loop(NT, lambda k: c_copy(k, (me + NT - k) % NT).wait_recv())
    for s in range(NT):
        dbc_ref[s * rows_each : (s + 1) * rows_each] = b_full[s].astype(F32)
    loop(NDP, lambda k: h_copy(k, (w + NDP - k) % NDP).wait_recv())
    for c in range(NDP):
        a, b = c // 4, c % 4
        qm_ref[a * 8 : (a + 1) * 8, b * BLK : (b + 1) * BLK] = q_full[c]

    for copy in sent:
        copy.wait_send()
    for s in range(NT):
        m_copy(s).wait()

    def finish_workers(k):
        pay_copy(k, w).wait_send()
        q_copy(k).wait_send()
        h_copy(k, w).wait_send()

    def finish_shards(k):
        s_copy(k).wait_send()
        b_copy(k).wait_send()
        c_copy(k, me).wait_send()

    loop(NDP, finish_workers)
    loop(NT, finish_shards)


def error_kernel(
    m_ref, ph_ref, qm_ref, dinp_ref, dbc_ref, ddt_ref, dgate_ref, pay_ref,
    out_ref, ph_out, qm_out, dinp_out, dbc_out, ddt_out, dgate_out, gain_out, skip_out, alog_out,
    right,
):
    b = pl.program_id(0)

    @pl.when(b == 0)
    def _():
        q_hi, q_lo = split2(-qm_ref[...])
        right[:RANK] = q_hi
        right[RANK : 2 * RANK] = q_lo
        right[2 * RANK :] = q_hi
        qm_out[...] = qm_ref[...]
        dinp_out[...] = dinp_ref[...]
        dbc_out[...] = dbc_ref[...]
        ddt_out[...] = ddt_ref[...]
        dgate_out[...] = dgate_ref[...]
        for p in range(HEADS // 2):
            gain_out[p * BLK : (p + 1) * BLK] = pay_ref[p]
            skips = pay_ref[4 + p : 5 + p, :]
            skip_out[2 * p] = jnp.sum(skips[:, :64])
            skip_out[2 * p + 1] = jnp.sum(skips[:, 64:])
        for h in range(HEADS):
            alog_out[h] = pay_ref[8 + h, 0]

    ph = ph_ref[...]
    ph_out[...] = ph
    hi, lo = split2(ph)
    left = jnp.concatenate([hi, hi, lo], axis=0)
    out_ref[...] = m_ref[...] + lax.dot_general(
        left, right[...], (((0,), (0,)), ((), ())), preferred_element_type=F32
    )


def vmem():
    return pl.BlockSpec(memory_space=pltpu.VMEM)


def smem():
    return pl.BlockSpec(memory_space=pltpu.SMEM)


def hbm():
    return pl.BlockSpec(memory_space=pl.ANY)


def shape(dims, dtype=F32):
    return jax.ShapeDtypeStruct(dims, dtype)


DMA = pltpu.SemaphoreType.DMA


def shards(
    layer_input, w_x, gate_in, bc, dt_raw, a_log, skip, gain, doc_ids, d_out, q_prev, error_in
):
    merged, ph, qm, d_input, d_bc, d_dt, d_gate, pay = pl.pallas_call(
        main_kernel,
        name="main",
        out_shape=(
            shape((D, CH)), shape((RANK, D)), shape((RANK, CH)), shape((T, CH), BF16),
            shape((T, 256)), shape((HEADS, T)), shape((T, CH), BF16), shape((16, BLK)),
        ),
        in_specs=[vmem(), hbm(), hbm()] + [vmem()] * 4 + [smem(), smem()] + [vmem()] * 3,
        out_specs=(hbm(),) + (vmem(),) * 7,
        scratch_shapes=[
            pltpu.VMEM((NT, T, CH), BF16),
            pltpu.VMEM((D, CH), BF16),
            pltpu.VMEM((D, CH), F32),
            pltpu.VMEM((RANK, D), F32),
            pltpu.VMEM((HEADS, T, T), BF16),
            pltpu.VMEM((HEADS, T, T), BF16),
            pltpu.VMEM((T, T), F32),
            pltpu.VMEM((T, T), F32),
            pltpu.VMEM((T, T), F32),
            pltpu.VMEM((T, T), F32),
            pltpu.VMEM((T, T), F32),
            pltpu.VMEM((HEADS, T), F32),
            pltpu.VMEM((HEADS, T), F32),
            pltpu.VMEM((HEADS, T), F32),
            pltpu.VMEM((HEADS, T), F32),
            pltpu.VMEM((T, CH), F32),
            pltpu.VMEM((T, CH), F32),
            pltpu.VMEM((T, CH), BF16),
            pltpu.VMEM((T, CH), BF16),
            pltpu.VMEM((T, CH), BF16),
            pltpu.VMEM((8, T), F32),
            pltpu.VMEM((NT, 8, T), F32),
            pltpu.VMEM((NDP, RANK, 256), F32),
            pltpu.VMEM((8, RANK, 256), F32),
            pltpu.VMEM((8, RANK, 256), F32),
            pltpu.VMEM((4, 2, RANK, 256), F32),
            pltpu.VMEM((2, RANK, 256), F32),
            pltpu.VMEM((RANK, 256), F32),
            pltpu.VMEM((NDP, RANK, 256), F32),
            pltpu.VMEM((2, T, CH), BF16),
            pltpu.VMEM((2, T, CH), BF16),
            pltpu.VMEM((2, HALF, CH), BF16),
            pltpu.VMEM((2, T, CH), BF16),
            pltpu.VMEM((2, HALF, CH), F32),
            pltpu.VMEM((2, T, CH), BF16),
            pltpu.VMEM((2, T, CH), BF16),
            pltpu.VMEM((2, HALF, CH), BF16),
            pltpu.VMEM((2, 2, HALF, CH), BF16),
            pltpu.VMEM((T, 256), F32),
            pltpu.VMEM((NT, T // NT, 256), BF16),
            pltpu.VMEM((NT, T // NT, 256), BF16),
            pltpu.VMEM((NT, T // NT, 256), BF16),
            pltpu.VMEM((16, BLK), F32),
            pltpu.VMEM((NDP, 16, BLK), F32),
            pltpu.VMEM((NDP, 8, BLK), F32),
            pltpu.VMEM((NDP, 8, BLK), F32),
            pltpu.VMEM((8, BLK), F32),
            pltpu.VMEM((NDP, 8, BLK), F32),
            DMA((3, NT, 2)), DMA((NT, 2)), DMA((NT,)), DMA((NT,)), DMA((NT,)), DMA((NT,)), DMA((NT,)),
            DMA((2,)), DMA((4,)), DMA((4,)), DMA((2,)), DMA((16,)), DMA((NDP,)),
            DMA((2,)), DMA((2,)), DMA((2,)), DMA((2,)), DMA((2,)), DMA((2,)), DMA((2, 2)), DMA((2, 2)),
            DMA((NT,)), DMA((NT,)), DMA((NT,)), DMA((NT,)),
            DMA((NDP,)), DMA((NDP,)), DMA((NDP,)), DMA((NDP,)), DMA((NDP,)), DMA((NDP,)),
        ],
        compiler_params=pltpu.CompilerParams(
            collective_id=0, has_side_effects=True, vmem_limit_bytes=VMEM_LIMIT
        ),
    )(
        layer_input, w_x, error_in, gate_in, d_out, bc, dt_raw, a_log, skip, gain, doc_ids, q_prev,
    )

    def whole(dims):
        return pl.BlockSpec(dims, lambda b: (0,) * len(dims))

    error_out, p_factor, right_mean, d_input, d_bc, d_dt, d_gate, d_gain, d_skip, d_alog = (
        pl.pallas_call(
            error_kernel,
            name="error",
            grid=(NT,),
            out_shape=(
                shape((D, CH)), shape((RANK, D)), shape((RANK, CH)), shape((T, CH), BF16),
                shape((T, 256)), shape((HEADS, T)), shape((T, CH), BF16), shape((CH,)),
                shape((HEADS,)), shape((HEADS,)),
            ),
            in_specs=[
                pl.BlockSpec((CH, CH), lambda b: (b, 0)),
                pl.BlockSpec((RANK, CH), lambda b: (0, b)),
                whole((RANK, CH)),
                whole((T, CH)),
                whole((T, 256)),
                whole((HEADS, T)),
                whole((T, CH)),
                whole((16, BLK)),
            ],
            out_specs=(
                pl.BlockSpec((CH, CH), lambda b: (b, 0)),
                pl.BlockSpec((RANK, CH), lambda b: (0, b)),
                whole((RANK, CH)),
                whole((T, CH)),
                whole((T, 256)),
                whole((HEADS, T)),
                whole((T, CH)),
                whole((CH,)),
                smem(),
                smem(),
            ),
            scratch_shapes=[pltpu.VMEM((3 * RANK, CH), BF16)],
            compiler_params=pltpu.CompilerParams(vmem_limit_bytes=VMEM_LIMIT),
        )(merged, ph, qm, d_input, d_bc, d_dt, d_gate, pay)
    )
    return (
        d_input, d_gate, d_bc, d_dt, d_alog, d_skip, d_gain, p_factor, right_mean, error_out,
    )


def solution(mesh):
    return jax.shard_map(
        shards,
        mesh=mesh,
        in_specs=(
            P("dp", "tensor"),
            P(None, "tensor"),
            P("dp", "tensor"),
            P("dp", None),
            P("tensor", "dp"),
            P("tensor"),
            P("tensor"),
            P("tensor"),
            P("dp"),
            P("dp", "tensor"),
            P(None, "tensor"),
            P("dp", "tensor"),
        ),
        out_specs=(
            P("dp", "tensor"),
            P("dp", "tensor"),
            P("dp", None),
            P("tensor", "dp"),
            P("tensor"),
            P("tensor"),
            P("tensor"),
            P("tensor", None),
            P(None, "tensor"),
            P("dp", "tensor"),
        ),
        check_vma=False,
    )
```

time: 143 us -> 99.3 us (0.69)
  Pallas kernels: 137 us -> 98.4 us
  local copies, waits for them, and re-layouts: 3.96 us -> 0 us
    pallas_call x2 -> x1, Pallas kernels: 125 us -> 87.4 us  [shards(): pl.pallas_call(main_kernel, name='main', out_shape=(shape((D, CH)), shape...]
    reshape x3 -> x0, local copies, waits for them, and re-layouts: 2.65 us -> none  [the longest x1 1.33 us: shards(): d_gain = pay[0:4].reshape(CH)]
where the time goes in v2:
time: 99.3 us; the launch traced here: 99 us
  Pallas kernels  98.4 us (99%)
    pallas_call x1, Pallas kernels, shards(): pl.pallas_call(main_kernel, name='main', out_shape=(shape((D, CH)), shape...  87.4 us
    pallas_call x1, Pallas kernels, shards(): pl.pallas_call(error_kernel, name='error', grid=(NT,), out_shape=(shape((...  10.9 us

profile of v2, /device:TPU:1, one launch (start us, length us, event | category | flops | bytes accessed | tf_op | source)
XLA Modules:
  0.0 99.0 jit_solution(16451387853918634681)
XLA Ops:
  0.6 87.4 %main.1 = (f32[4096,512]{1,0:T(8,128)}, f32[32,4096]{1,0:T(8,128)}, f32[32,512]{1,0:T(8,128)}, bf16[384,512]{1,0:T(8,128)(2,1)}, f32[384,256]{1,0:T(8,128)}, /*i...) custom-call(bf16[384,512]{1,0:T(8,128)(2,1)} %x_ref.1, bf16[4096,512]{1,0:T(8,128)(2,1)} %wx_hbm.1, ...), custom_call_target="tpu_custom_call" | custom-call | tf_op jit(solution)/shard_map/main/pallas_call | solution.py:721
  88.1 10.9 %error.1 = (f32[4096,512]{1,0:T(8,128)}, f32[32,4096]{1,0:T(8,128)}, f32[32,512]{1,0:T(8,128)}, bf16[384,512]{1,0:T(8,128)(2,1)}, f32[384,256]{1,0:T(8,128)}, /*...) custom-call(f32[4096,512]{1,0:T(8,128)} %get-tuple-element.28.m_ref, ...), custom_call_target="tpu_custom_call" | custom-call | tf_op jit(solution)/shard_map/error/pallas_call | solution.py:796

commit v3 on v2

--- a/solution.py
+++ b/solution.py
@@ -21,7 +21,10 @@
 BLK = 128
 NB = T // BLK
 LOW = -1e30
-VMEM_LIMIT = 56 * 1024 * 1024
+MAIN_VMEM = 46 * 1024 * 1024
+LAST_VMEM = 20 * 1024 * 1024
+ROWS = 1024
+FAR = (5, 3, 4, 7, 1, 6, 2)
 
 
 def dot_nn(a, b):
@@ -81,19 +84,19 @@
 
 
 def main_kernel(
-    x_ref, wx_hbm, e_hbm, gate_ref, dout_ref, bc_ref, dt_ref, alog_ref, skip_ref, gain_ref,
+    x_hbm, wx_hbm, e_hbm, gate_hbm, dout_hbm, bc_ref, dt_ref, alog_ref, skip_ref, gain_ref,
     doc_ref, q_ref,
-    m_hbm, ph_ref, qm_ref, dinp_ref, dbc_ref, ddt_ref, dgate_ref, pay_ref,
-    xall, wx, e_all, eq_ref, w_mat, wt_mat, bias, bias_t, scores, scores_t, d_scores,
+    e_all, ph_ref, qm_ref, dinp_ref, dbc_ref, ddt_ref, dgate_ref, pay_ref,
+    xall, gate_ref, dout_ref, wx, eq_ref, w_mat, wt_mat, bias, bias_t, scores, scores_t, d_scores,
     cum_ref, rowp_ref, row_sum, col_sum, acc, y_buf, inner_ref, dxb_ref, dy_ref, sums, sums_in,
-    p_send, core_in, p_mid, y_in, p_low, x_in, p_full,
+    p_send, core_in, p_mid, y_in, p_low, x_in, p_full, p_three, grams, m_hi, m_lo,
     dx_out, part_out, opp_out, near_out, near_hold, dx_in, part_in, opp_in, near_in,
-    bc_part, b_out, b_in, b_full, pay, pay_in, q_out, q_in, q_own, q_full,
-    x_send, x_recv, s_send, s_recv, wx_sem, e_sem, m_sem,
+    bc_part, b_out, b_in, b_full, pay, pay_in, pay_all, pay_full, q_out, q_in, q_all, q_full,
+    x_send, x_recv, s_send, s_recv, wx_sem, e_sem, in_sem,
     core_sem, y_send, y_recv, low_sem, g_send, g_recv,
     dx_send, dx_recv, part_send, part_recv, opp_send, opp_recv, near_send, near_recv,
     bs_sem, br_sem, cs_sem, cr_sem,
-    ys_sem, yr_sem, qs_sem, qr_sem, hs_sem, hr_sem,
+    ys_sem, yr_sem, pay_sem, qs_sem, qr_sem, q_sem,
 ):
     me = lax.axis_index("tensor")
     z = me // 2
@@ -108,10 +111,14 @@
     xh = (w // 2) % 2
     y = w // 4
     other_core = w + 1 - 2 * core
+    place = y * 2 + xh
     other_x = w + 2 - 4 * xh
 
     def y_peer(k):
         return ((y + k) % 4) * 4 + xh * 2 + core
+
+    def same_core(k):
+        return ((place + k) % 8) * 2 + core
 
     def loop(count, step_body):
         def step(k, carry):
@@ -136,12 +143,16 @@
         rows = pl.ds(b * CH, CH)
         return pltpu.make_async_copy(e_hbm.at[rows], e_all.at[rows], e_sem.at[b])
 
+    own_load = pltpu.make_async_copy(x_hbm, xall.at[me], in_sem.at[0])
+    gate_load = pltpu.make_async_copy(gate_hbm, gate_ref, in_sem.at[1])
+    dout_load = pltpu.make_async_copy(dout_hbm, dout_ref, in_sem.at[2])
+    own_load.start()
     for b in range(NT):
         e_copy(b).start()
     for b in range(NT):
         wx_copy(b).start()
-
-    xall[me] = x_ref[...]
+    gate_load.start()
+    dout_load.start()
     pl.semaphore_wait(barrier, NT - 1 + NDP - 1)
 
     def x_copy(way, to, src, half):
@@ -162,13 +173,26 @@
         copy.start()
         sent.append(copy)
 
+    def send_own(way, to, half):
+        rows = pl.ds(half * HALF, HALF)
+        copy = pltpu.make_async_remote_copy(
+            src_ref=x_hbm.at[rows],
+            dst_ref=xall.at[me, rows],
+            send_sem=x_send.at[way, me, half],
+            recv_sem=x_recv.at[me, half],
+            device_id={"tensor": to},
+            device_id_type=MESH,
+        )
+        copy.start()
+        sent.append(copy)
+
     def arrive(src, half):
         x_copy(0, zp, src, half).wait_recv()
 
     for half in range(2):
-        send(0, zp, me, half)
-        send(1, zm, me, half)
-        send(2, xp, me, half)
+        send_own(0, zp, half)
+        send_own(1, zm, 1 - half)
+        send_own(2, xp, half)
 
     step = softplus(dt_ref[...])
     rate = head_rates(alog_ref) * step
@@ -191,14 +215,18 @@
         both = dot_nt(q_two, e_hi)
         eq_ref[:, b * CH : (b + 1) * CH] = both[:RANK] + both[RANK:] + dot_nt(q_hi, e_lo)
 
-    for b in range(NT):
+    for b in range(5):
         e_block(b)
 
     arrive(zm, 0)
     send(0, zp, zm, 0)
+    arrive(zp, 1)
+    send(1, zm, zp, 1)
     arrive(xp, 0)
     send(0, zp, xp, 0)
     send(1, zm, xp, 0)
+    for b in range(5, NT):
+        e_block(b)
 
     def weights(h, carry):
         cum_row = cum_ref[pl.ds(h, 1), :]
@@ -219,8 +247,6 @@
 
     lax.fori_loop(0, HEADS, weights, 0)
 
-    arrive(zp, 1)
-    send(1, zm, zp, 1)
     arrive(xp, 1)
     send(0, zp, xp, 1)
     send(1, zm, xp, 1)
@@ -234,6 +260,7 @@
         rows = pl.ds(pl.multiple_of(src * CH, CH), CH)
         return dot_nn(xall[src], wx[rows, :])
 
+    own_load.wait()
     acc[...] = product(me) + product(xp)
     acc[...] += product(zm) + product(zp)
     arrive(zo, 0)
@@ -249,6 +276,8 @@
         arrive(other, 1)
         acc[...] += product(other)
     inner_ref[...] = acc[...].astype(BF16)
+    gate_load.wait()
+    dout_load.wait()
 
     low_lanes = iota((1, BLK), 1) < 64
 
@@ -345,6 +374,35 @@
         sent.append(copy)
 
     dxb = dxb_ref[...]
+
+    def input_part(s):
+        rows = pl.ds(pl.multiple_of(s * CH, CH), CH)
+        return dot_nt(dxb, wx[rows, :])
+
+    def dx_copy(i):
+        return remote(dx_out.at[i], dx_in.at[i], dx_send.at[i], dx_recv.at[i], "tensor", xp)
+
+    ways = (zp, zm)
+
+    def part_copy(i):
+        return remote(
+            part_out.at[i], part_in.at[i], part_send.at[i], part_recv.at[i], "tensor", ways[i]
+        )
+
+    def opp_copy(i):
+        return remote(
+            opp_out.at[i], opp_in.at[i], opp_send.at[i], opp_recv.at[i], "tensor", ways[i]
+        )
+
+    def near_copy(i, half):
+        return remote(
+            near_out.at[i, pl.ds(half * HALF, HALF)], near_in.at[i, half],
+            near_send.at[i, half], near_recv.at[i, half], "tensor", ways[i],
+        )
+
+    dx_out[0] = input_part(xp_zo).astype(BF16)
+    begin(dx_copy(0))
+
     q3 = jnp.concatenate(split3(q_ref[...]), axis=0)
     z3 = dot_nt(q3, dxb)
     z_sum = z3[:RANK] + z3[RANK : 2 * RANK] + z3[2 * RANK :]
@@ -361,33 +419,6 @@
     )
     begin(core_copy)
 
-    def input_part(s):
-        rows = pl.ds(pl.multiple_of(s * CH, CH), CH)
-        return dot_nt(dxb, wx[rows, :])
-
-    def dx_copy(i):
-        return remote(dx_out.at[i], dx_in.at[i], dx_send.at[i], dx_recv.at[i], "tensor", xp)
-
-    ways = (zp, zm)
-
-    def part_copy(i):
-        return remote(
-            part_out.at[i], part_in.at[i], part_send.at[i], part_recv.at[i], "tensor", ways[i]
-        )
-
-    def opp_copy(i):
-        return remote(
-            opp_out.at[i], opp_in.at[i], opp_send.at[i], opp_recv.at[i], "tensor", ways[i]
-        )
-
-    def near_copy(i, half):
-        return remote(
-            near_out.at[i, pl.ds(half * HALF, HALF)], near_in.at[i, half],
-            near_send.at[i, half], near_recv.at[i, half], "tensor", ways[i],
-        )
-
-    dx_out[0] = input_part(xp_zo).astype(BF16)
-    begin(dx_copy(0))
     part_out[0] = input_part(xp_zp).astype(BF16)
     begin(part_copy(0))
     part_out[1] = input_part(xp_zm).astype(BF16)
@@ -403,7 +434,7 @@
             p_mid.at[pl.ds((to // 4) * 2, 2)], y_in.at[k], y_send.at[k], y_recv.at[k], "dp", to
         )
 
-    for k in range(1, 4):
+    for k in (2, 1, 3):
         begin(y_copy(k))
 
     to_zp = input_part(zp)
@@ -444,19 +475,20 @@
             for j in range(NB):
                 col_sum[h : h + 1, j * BLK : (j + 1) * BLK] = downs[j]
 
-    def m_copy(s):
-        rows = pl.ds(s * CH, CH)
-        return pltpu.make_async_copy(e_all.at[rows], m_hbm.at[rows], m_sem.at[s])
-
     def merge(s):
         rows = slice(s * CH, (s + 1) * CH)
-        e_all[rows] += lax.dot_general(
+        total = e_all[rows] + lax.dot_general(
             xall[s], dxb_ref[...], (((0,), (0,)), ((), ())), preferred_element_type=F32
         )
-        m_copy(s).start()
+        e_all[rows] = total
+        hi, lo = split2(total)
+        m_hi[rows] = hi
+        m_lo[rows] = lo
 
     head_back(0)
+    head_back(1)
     merge(0)
+    merge(1)
     for k in range(1, 4):
         y_copy(k).wait_recv()
     for c in range(2):
@@ -464,31 +496,46 @@
     low_copy = remote(p_low.at[1 - xh], x_in, low_sem.at[0], low_sem.at[1], "dp", other_x)
     begin(low_copy)
 
-    head_back(1)
-    merge(1)
-    low_copy.wait_recv()
-    mine = core * 8 + y * 2 + xh
-    p_full[mine] = (p_low[xh] + x_in[...]) / NDP
-
-    def g_copy(chunk, to, n):
-        return remote(
-            p_full.at[chunk], p_full.at[chunk], g_send.at[n], g_recv.at[chunk], "dp", to
-        )
-
-    begin(g_copy(mine, other_x, 0))
-    for k in range(1, 4):
-        begin(g_copy(mine, y_peer(k), k))
-    begin(g_copy(mine, other_core, 4))
-
     dx_copy(0).wait_recv()
     opposite = input_part(zo) + dx_in[0].astype(F32)
     for i in range(2):
         opp_out[i] = opposite[i * HALF : (i + 1) * HALF].astype(BF16)
         begin(opp_copy(i))
 
+    head_back(2)
+    mine = core * 8 + place
+    low_copy.wait_recv()
+    p_full[mine] = (p_low[xh] + x_in[...]) / NDP
+
+    def g_copy(chunk, to, n):
+        return remote(
+            p_full.at[chunk], p_full.at[chunk], g_send.at[n], g_recv.at[chunk], "dp", to
+        )
+
+    begin(g_copy(mine, other_x, 0))
+    for k in (2, 1, 3):
+        begin(g_copy(mine, y_peer(k), k))
+    begin(g_copy(mine, other_core, 4))
+
+    def gram_one(c):
+        three = jnp.concatenate(split3(p_full[c]), axis=0)
+        p_three[c] = three
+        g9 = dot_nt(three, three)
+        g3 = g9[:RANK] + g9[RANK : 2 * RANK] + g9[2 * RANK :]
+        grams[c] = g3[:, :RANK] + g3[:, RANK : 2 * RANK] + g3[:, 2 * RANK :]
+
+    gram_one(mine)
+    head_back(3)
+
+    bc_part[:, :128] = dot_nn(d_scores[...].T.astype(BF16), c_part)
+    bc_part[:, 128:] = dot_nn(d_scores[...].astype(BF16), b_part)
+    rows_each = T // NT
+    for s in range(NT):
+        b_out[s] = bc_part[s * rows_each : (s + 1) * rows_each].astype(BF16)
+
     across_x = core * 8 + y * 2 + 1 - xh
     g_copy(across_x, other_x, 0).wait_recv()
-    for k in range(1, 4):
+    for k in (2, 1, 3):
         begin(g_copy(across_x, y_peer(k), 4 + k))
     begin(g_copy(across_x, other_core, 8))
 
@@ -498,36 +545,67 @@
         input_part(xp) + part_in[0].astype(F32) + part_in[1].astype(F32)
     ).astype(BF16)
     begin(dx_copy(1))
-
-    for k in range(1, 4):
+    gram_one(across_x)
+
+    lower = (iota((T, T), 0) >= iota((T, T), 1)).astype(F32)
+    columns = col_sum[...]
+    d_rate = jnp.dot(columns - row_sum[...], lower, precision=HIGH, preferred_element_type=F32)
+    raw = dt_ref[...]
+    step = softplus(raw)
+    decay = head_rates(alog_ref)
+    d_step = columns / step + decay * d_rate
+    ddt_ref[...] = d_step / (1.0 + jnp.exp(-raw))
+    pay[8:16, :] = jnp.broadcast_to(
+        jnp.sum(d_rate * decay * step, axis=1, keepdims=True), (HEADS, BLK)
+    )
+
+    pay_core = remote(
+        pay.at[pl.ds((1 - core) * 8, 8)], pay_in, pay_sem.at[0], pay_sem.at[1], "dp", other_core
+    )
+    begin(pay_core)
+    for s in range(2, 5):
+        merge(s)
+
+    for k in (1, 3, 2):
         for c in range(2):
             chunk = core * 8 + ((y + k) % 4) * 2 + c
             g_copy(chunk, other_core, 0).wait_recv()
             begin(g_copy(chunk, other_core, 7 + 2 * k + c))
-
-    head_back(2)
-    head_back(3)
-    for s in range(2, NT):
-        merge(s)
+            gram_one(chunk)
+
+    pay_core.wait_recv()
+    pay_all[place] = pay[pl.ds(core * 8, 8), :] + pay_in[...]
+
+    def pay_copy(k, slot):
+        return remote(
+            pay_all.at[slot], pay_all.at[slot], ys_sem.at[k], yr_sem.at[k], "dp", same_core(k)
+        )
+
+    for k in FAR:
+        begin(pay_copy(k, place))
 
     for i in range(2):
-        half = i
-        rows = slice(half * HALF, (half + 1) * HALF)
+        rows = slice(i * HALF, (i + 1) * HALF)
         opp_copy(i).wait_recv()
         near_out[i, rows] = (near_hold[i] + opp_in[i].astype(F32)).astype(BF16)
-        begin(near_copy(i, half))
+        begin(near_copy(i, i))
+
+    def b_copy(k):
+        to = (me + k) % NT
+        return remote(b_out.at[to], b_in.at[k], bs_sem.at[k], br_sem.at[k], "tensor", to)
+
+    loop(NT, lambda k: b_copy(k).start())
+    for s in range(5, NT):
+        merge(s)
 
     for c in range(8):
         chunk = (1 - core) * 8 + c
         g_copy(chunk, other_core, 0).wait_recv()
-
-    def gram_add(c, total):
-        three = jnp.concatenate(split3(p_full[c]), axis=0)
-        return total + dot_nt(three, three)
-
-    g9 = lax.fori_loop(0, NDP, gram_add, jnp.zeros((3 * RANK, 3 * RANK), F32))
-    g3 = g9[:RANK] + g9[RANK : 2 * RANK] + g9[2 * RANK :]
-    gram = g3[:, :RANK] + g3[:, RANK : 2 * RANK] + g3[:, 2 * RANK :]
+        gram_one(chunk)
+
+    gram = grams[0]
+    for c in range(1, NDP):
+        gram = gram + grams[c]
     eye = (iota((RANK, RANK), 0) == iota((RANK, RANK), 1)).astype(F32)
     table = jnp.concatenate([eye, gram], axis=1)
     places = iota((RANK, 2 * RANK), 0)
@@ -539,72 +617,43 @@
     pivots = jnp.sum(jnp.where(eye > 0.0, table[:, RANK:], 0.0), axis=1, keepdims=True)
     inverse = table[:, :RANK] * lax.rsqrt(pivots)
 
-    for c in range(NDP):
-        ph_ref[:, c * 256 : (c + 1) * 256] = jnp.dot(
-            inverse, p_full[c], precision=HIGH, preferred_element_type=F32
-        )
-
-    def q_part(s, total):
-        lanes = pl.ds(pl.multiple_of(s * CH, CH), CH)
-        hi, lo = split2(ph_ref[:, lanes])
-        two = jnp.concatenate([hi, lo], axis=0)
-        m_hi, m_lo = split2(e_all[lanes, :])
-        both = dot_nn(two, m_hi)
-        return total + both[:RANK] + both[RANK:] + dot_nn(hi, m_lo)
-
-    q_local = lax.fori_loop(0, NT, q_part, jnp.zeros((RANK, CH), F32))
-    for c in range(NDP):
-        a, b = c // 4, c % 4
-        q_out[c] = q_local[a * 8 : (a + 1) * 8, b * BLK : (b + 1) * BLK]
-
-    def q_copy(k):
-        to = (w + k) % NDP
-        return remote(q_out.at[to], q_in.at[k], qs_sem.at[k], qr_sem.at[k], "dp", to)
-
-    loop(NDP, lambda k: q_copy(k).start())
-
-    bc_part[:, :128] = dot_nn(d_scores[...].T.astype(BF16), c_part)
-    bc_part[:, 128:] = dot_nn(d_scores[...].astype(BF16), b_part)
-    rows_each = T // NT
+    i_hi, i_mid, i_lo = split3(inverse)
+    none = jnp.zeros_like(i_hi)
+    left = jnp.concatenate(
+        [
+            jnp.concatenate([i_hi, i_hi, i_hi], axis=1),
+            jnp.concatenate([i_mid, i_mid, none], axis=1),
+            jnp.concatenate([i_lo, none, none], axis=1),
+        ],
+        axis=0,
+    )
+    q_local = jnp.zeros((RANK, CH), F32)
     for s in range(NT):
-        b_out[s] = bc_part[s * rows_each : (s + 1) * rows_each].astype(BF16)
-
-    def b_copy(k):
-        to = (me + k) % NT
-        return remote(b_out.at[to], b_in.at[k], bs_sem.at[k], br_sem.at[k], "tensor", to)
-
-    loop(NT, lambda k: b_copy(k).start())
-
-    lower = (iota((T, T), 0) >= iota((T, T), 1)).astype(F32)
-    columns = col_sum[...]
-    d_rate = jnp.dot(columns - row_sum[...], lower, precision=HIGH, preferred_element_type=F32)
-    raw = dt_ref[...]
-    step = softplus(raw)
-    decay = head_rates(alog_ref)
-    d_step = columns / step + decay * d_rate
-    ddt_ref[...] = d_step / (1.0 + jnp.exp(-raw))
-    pay[8:16, :] = jnp.broadcast_to(
-        jnp.sum(d_rate * decay * step, axis=1, keepdims=True), (HEADS, BLK)
-    )
-    pay_in[w] = pay[...]
-
-    def pay_copy(k, slot):
-        return remote(pay, pay_in.at[slot], ys_sem.at[k], yr_sem.at[k], "dp", (w + k) % NDP)
-
-    loop(NDP, lambda k: pay_copy(k, w).start())
-
-    def q_add(k, total):
-        q_copy(k).wait_recv()
-        return total + q_in[k]
-
-    q_sum = lax.fori_loop(1, NDP, q_add, q_out[w]) / NDP
-    q_own[...] = q_sum
-    q_full[w] = q_sum
-
-    def h_copy(k, slot):
-        return remote(q_own, q_full.at[slot], hs_sem.at[k], hr_sem.at[k], "dp", (w + k) % NDP)
-
-    loop(NDP, lambda k: h_copy(k, w).start())
+        blocks = []
+        for c in (2 * s, 2 * s + 1):
+            three = dot_nn(left, p_three[c])
+            blocks.append(three[:RANK] + three[RANK : 2 * RANK] + three[2 * RANK :])
+        ph = jnp.concatenate(blocks, axis=1)
+        rows = slice(s * CH, (s + 1) * CH)
+        ph_ref[:, rows] = ph
+        hi, lo = split2(ph)
+        both = dot_nn(jnp.concatenate([hi, lo], axis=0), m_hi[rows])
+        q_local = q_local + both[:RANK] + both[RANK:] + dot_nn(hi, m_lo[rows])
+
+    for c in range(2):
+        q_out[c] = q_local[c * 16 : (c + 1) * 16]
+    q_core = remote(q_out.at[1 - core], q_in, q_sem.at[0], q_sem.at[1], "dp", other_core)
+    begin(q_core)
+    q_core.wait_recv()
+    q_all[place] = q_out[core] + q_in[...]
+
+    def q_copy(k, slot):
+        return remote(
+            q_all.at[slot], q_all.at[slot], qs_sem.at[k], qr_sem.at[k], "dp", same_core(k)
+        )
+
+    for k in FAR:
+        begin(q_copy(k, place))
 
     def b_add(k, total):
         b_copy(k).wait_recv()
@@ -632,32 +681,49 @@
             + dx_in[1, rows].astype(F32)
         ).astype(BF16)
 
-    loop(NDP, lambda k: pay_copy(k, (w + NDP - k) % NDP).wait_recv())
-    pay_ref[...] = lax.fori_loop(1, NDP, lambda c, t: t + pay_in[c], pay_in[0])
+    for k in range(1, 8):
+        q_copy(k, (place + 8 - k) % 8).wait_recv()
+    q_sum = q_all[0]
+    for c in range(1, 8):
+        q_sum = q_sum + q_all[c]
+    q_full[core] = q_sum / NDP
+    q_back = remote(
+        q_full.at[core], q_full.at[core], q_sem.at[2], q_sem.at[3], "dp", other_core
+    )
+    begin(q_back)
+
+    for k in range(1, 8):
+        pay_copy(k, (place + 8 - k) % 8).wait_recv()
+    pay_sum = pay_all[0]
+    for c in range(1, 8):
+        pay_sum = pay_sum + pay_all[c]
+    pay_full[core] = pay_sum
+    pay_back = remote(
+        pay_full.at[core], pay_full.at[core], pay_sem.at[2], pay_sem.at[3], "dp", other_core
+    )
+    begin(pay_back)
     loop(NT, lambda k: c_copy(k, (me + NT - k) % NT).wait_recv())
     for s in range(NT):
         dbc_ref[s * rows_each : (s + 1) * rows_each] = b_full[s].astype(F32)
-    loop(NDP, lambda k: h_copy(k, (w + NDP - k) % NDP).wait_recv())
-    for c in range(NDP):
-        a, b = c // 4, c % 4
-        qm_ref[a * 8 : (a + 1) * 8, b * BLK : (b + 1) * BLK] = q_full[c]
+    remote(
+        q_full.at[1 - core], q_full.at[1 - core], q_sem.at[2], q_sem.at[3], "dp", other_core
+    ).wait_recv()
+    remote(
+        pay_full.at[1 - core], pay_full.at[1 - core], pay_sem.at[2], pay_sem.at[3], "dp", other_core
+    ).wait_recv()
+    for c in range(2):
+        pay_ref[c * 8 : (c + 1) * 8] = pay_full[c]
+    for c in range(2):
+        qm_ref[c * 16 : (c + 1) * 16] = q_full[c]
 
     for copy in sent:
         copy.wait_send()
-    for s in range(NT):
-        m_copy(s).wait()
-
-    def finish_workers(k):
-        pay_copy(k, w).wait_send()
-        q_copy(k).wait_send()
-        h_copy(k, w).wait_send()
 
     def finish_shards(k):
         s_copy(k).wait_send()
         b_copy(k).wait_send()
         c_copy(k, me).wait_send()
 
-    loop(NDP, finish_workers)
     loop(NT, finish_shards)
 
 
@@ -687,11 +753,12 @@
         for h in range(HEADS):
             alog_out[h] = pay_ref[8 + h, 0]
 
-    ph = ph_ref[...]
+    rows = pl.ds(pl.multiple_of(b * ROWS, ROWS), ROWS)
+    ph = ph_ref[:, rows]
     ph_out[...] = ph
     hi, lo = split2(ph)
     left = jnp.concatenate([hi, hi, lo], axis=0)
-    out_ref[...] = m_ref[...] + lax.dot_general(
+    out_ref[...] = m_ref[rows, :] + lax.dot_general(
         left, right[...], (((0,), (0,)), ((), ())), preferred_element_type=F32
     )
 
@@ -706,6 +773,14 @@
 
 def hbm():
     return pl.BlockSpec(memory_space=pl.ANY)
+
+
+def in_vmem(array):
+    return pltpu.with_memory_space_constraint(array, pltpu.VMEM)
+
+
+def in_hbm(array):
+    return pltpu.with_memory_space_constraint(array, pltpu.HBM)
 
 
 def shape(dims, dtype=F32):
@@ -722,15 +797,17 @@
         main_kernel,
         name="main",
         out_shape=(
-            shape((D, CH)), shape((RANK, D)), shape((RANK, CH)), shape((T, CH), BF16),
-            shape((T, 256)), shape((HEADS, T)), shape((T, CH), BF16), shape((16, BLK)),
+            pltpu.VMEM((D, CH), F32), pltpu.VMEM((RANK, D), F32), pltpu.VMEM((RANK, CH), F32),
+            pltpu.VMEM((T, CH), BF16), pltpu.VMEM((T, 256), F32), pltpu.VMEM((HEADS, T), F32),
+            pltpu.VMEM((T, CH), BF16), pltpu.VMEM((16, BLK), F32),
         ),
-        in_specs=[vmem(), hbm(), hbm()] + [vmem()] * 4 + [smem(), smem()] + [vmem()] * 3,
-        out_specs=(hbm(),) + (vmem(),) * 7,
+        in_specs=[hbm()] * 5 + [vmem()] * 2 + [smem(), smem()] + [vmem()] * 3,
+        out_specs=(vmem(),) * 8,
         scratch_shapes=[
             pltpu.VMEM((NT, T, CH), BF16),
+            pltpu.VMEM((T, CH), BF16),
+            pltpu.VMEM((T, CH), BF16),
             pltpu.VMEM((D, CH), BF16),
-            pltpu.VMEM((D, CH), F32),
             pltpu.VMEM((RANK, D), F32),
             pltpu.VMEM((HEADS, T, T), BF16),
             pltpu.VMEM((HEADS, T, T), BF16),
@@ -757,6 +834,10 @@
             pltpu.VMEM((2, RANK, 256), F32),
             pltpu.VMEM((RANK, 256), F32),
             pltpu.VMEM((NDP, RANK, 256), F32),
+            pltpu.VMEM((NDP, 3 * RANK, 256), BF16),
+            pltpu.VMEM((NDP, RANK, RANK), F32),
+            pltpu.VMEM((D, CH), BF16),
+            pltpu.VMEM((D, CH), BF16),
             pltpu.VMEM((2, T, CH), BF16),
             pltpu.VMEM((2, T, CH), BF16),
             pltpu.VMEM((2, HALF, CH), BF16),
@@ -771,22 +852,25 @@
             pltpu.VMEM((NT, T // NT, 256), BF16),
             pltpu.VMEM((NT, T // NT, 256), BF16),
             pltpu.VMEM((16, BLK), F32),
-            pltpu.VMEM((NDP, 16, BLK), F32),
-            pltpu.VMEM((NDP, 8, BLK), F32),
-            pltpu.VMEM((NDP, 8, BLK), F32),
             pltpu.VMEM((8, BLK), F32),
-            pltpu.VMEM((NDP, 8, BLK), F32),
-            DMA((3, NT, 2)), DMA((NT, 2)), DMA((NT,)), DMA((NT,)), DMA((NT,)), DMA((NT,)), DMA((NT,)),
+            pltpu.VMEM((8, 8, BLK), F32),
+            pltpu.VMEM((2, 8, BLK), F32),
+            pltpu.VMEM((2, RANK // 2, CH), F32),
+            pltpu.VMEM((RANK // 2, CH), F32),
+            pltpu.VMEM((8, RANK // 2, CH), F32),
+            pltpu.VMEM((2, RANK // 2, CH), F32),
+            DMA((3, NT, 2)), DMA((NT, 2)), DMA((NT,)), DMA((NT,)), DMA((NT,)), DMA((NT,)), DMA((3,)),
             DMA((2,)), DMA((4,)), DMA((4,)), DMA((2,)), DMA((16,)), DMA((NDP,)),
             DMA((2,)), DMA((2,)), DMA((2,)), DMA((2,)), DMA((2,)), DMA((2,)), DMA((2, 2)), DMA((2, 2)),
             DMA((NT,)), DMA((NT,)), DMA((NT,)), DMA((NT,)),
-            DMA((NDP,)), DMA((NDP,)), DMA((NDP,)), DMA((NDP,)), DMA((NDP,)), DMA((NDP,)),
+            DMA((8,)), DMA((8,)), DMA((4,)), DMA((8,)), DMA((8,)), DMA((4,)),
         ],
         compiler_params=pltpu.CompilerParams(
-            collective_id=0, has_side_effects=True, vmem_limit_bytes=VMEM_LIMIT
+            collective_id=0, has_side_effects=True, vmem_limit_bytes=MAIN_VMEM
         ),
     )(
-        layer_input, w_x, error_in, gate_in, d_out, bc, dt_raw, a_log, skip, gain, doc_ids, q_prev,
+        in_hbm(layer_input), in_hbm(w_x), in_hbm(error_in), in_hbm(gate_in), in_hbm(d_out),
+        in_hbm(bc), in_hbm(dt_raw), a_log, skip, in_hbm(gain), in_hbm(doc_ids), in_hbm(q_prev),
     )
 
     def whole(dims):
@@ -796,25 +880,16 @@
         pl.pallas_call(
             error_kernel,
             name="error",
-            grid=(NT,),
+            grid=(D // ROWS,),
             out_shape=(
                 shape((D, CH)), shape((RANK, D)), shape((RANK, CH)), shape((T, CH), BF16),
                 shape((T, 256)), shape((HEADS, T)), shape((T, CH), BF16), shape((CH,)),
                 shape((HEADS,)), shape((HEADS,)),
             ),
-            in_specs=[
-                pl.BlockSpec((CH, CH), lambda b: (b, 0)),
-                pl.BlockSpec((RANK, CH), lambda b: (0, b)),
-                whole((RANK, CH)),
-                whole((T, CH)),
-                whole((T, 256)),
-                whole((HEADS, T)),
-                whole((T, CH)),
-                whole((16, BLK)),
-            ],
+            in_specs=[vmem()] * 8,
             out_specs=(
-                pl.BlockSpec((CH, CH), lambda b: (b, 0)),
-                pl.BlockSpec((RANK, CH), lambda b: (0, b)),
+                pl.BlockSpec((ROWS, CH), lambda b: (b, 0)),
+                pl.BlockSpec((RANK, ROWS), lambda b: (0, b)),
                 whole((RANK, CH)),
                 whole((T, CH)),
                 whole((T, 256)),
@@ -825,8 +900,11 @@
                 smem(),
             ),
             scratch_shapes=[pltpu.VMEM((3 * RANK, CH), BF16)],
-            compiler_params=pltpu.CompilerParams(vmem_limit_bytes=VMEM_LIMIT),
-        )(merged, ph, qm, d_input, d_bc, d_dt, d_gate, pay)
+            compiler_params=pltpu.CompilerParams(vmem_limit_bytes=LAST_VMEM),
+        )(
+            in_vmem(merged), in_vmem(ph), in_vmem(qm), in_vmem(d_input), in_vmem(d_bc),
+            in_vmem(d_dt), in_vmem(d_gate), in_vmem(pay),
+        )
     )
     return (
         d_input, d_gate, d_bc, d_dt, d_alog, d_skip, d_gain, p_factor, right_mean, error_out,

time: 99.3 us -> 87.4 us (0.88)
  Pallas kernels: 98.4 us -> 86.7 us
    pallas_call x2, Pallas kernels: 98.4 us -> 86.7 us  [the longest x1 81.8 us: shards(): pl.pallas_call(main_kernel, name='main', out_shape=(pltpu.VMEM((D, CH), F...]
where the time goes in v3:
time: 87.4 us; the launch traced here: 87.3 us
  Pallas kernels  86.7 us (99%)
    pallas_call x1, Pallas kernels, shards(): pl.pallas_call(main_kernel, name='main', out_shape=(pltpu.VMEM((D, CH), F...  81.8 us
    pallas_call x1, Pallas kernels, shards(): pl.pallas_call(error_kernel, name='error', grid=(D // ROWS,), out_shape=(...  4.86 us

profile of v3, /device:TPU:1, one launch (start us, length us, event | category | flops | bytes accessed | tf_op | source)
XLA Modules:
  0.0 87.3 jit_solution(3860592889242171940)
XLA Ops:
  0.6 81.8 %main.1 = (f32[4096,512]{1,0:T(8,128)S(1)}, f32[32,4096]{1,0:T(8,128)S(1)}, f32[32,512]{1,0:T(8,128)S(1)}, bf16[384,512]{1,0:T(8,128)(2,1)S(1)}, f32[384,256]{1,...) custom-call(bf16[384,512]{1,0:T(8,128)(2,1)} %x_hbm.1, ...), custom_call_target="tpu_custom_call" | custom-call | tf_op jit(solution)/shard_map/main/pallas_call | solution.py:796
  82.5 4.9 %error.1 = (f32[4096,512]{1,0:T(8,128)}, f32[32,4096]{1,0:T(8,128)}, f32[32,512]{1,0:T(8,128)}, bf16[384,512]{1,0:T(8,128)(2,1)}, f32[384,256]{1,0:T(8,128)}, /*...) custom-call(f32[4096,512]{1,0:T(8,128)S(1)} %get-tuple-element.28.m_ref, ...), custom_call_target="tpu_custom_call" | custom-call | tf_op jit(solution)/shard_map/error/pallas_call | solution.py:880

commit v4 on v3

--- a/solution.py
+++ b/solution.py
@@ -12,6 +12,7 @@
 BF16 = jnp.bfloat16
 T = 384
 HALF = T // 2
+QUARTER = T // 4
 HEADS = 8
 CH = 512
 NT = 8
@@ -89,7 +90,7 @@
     e_all, ph_ref, qm_ref, dinp_ref, dbc_ref, ddt_ref, dgate_ref, pay_ref,
     xall, gate_ref, dout_ref, wx, eq_ref, w_mat, wt_mat, bias, bias_t, scores, scores_t, d_scores,
     cum_ref, rowp_ref, row_sum, col_sum, acc, y_buf, inner_ref, dxb_ref, dy_ref, sums, sums_in,
-    p_send, core_in, p_mid, y_in, p_low, x_in, p_full, p_three, grams, m_hi, m_lo,
+    p_send, core_in, p_mid, y_in, p_low, x_in, p_full, p_three, s_acc, m_hi, m_lo,
     dx_out, part_out, opp_out, near_out, near_hold, dx_in, part_in, opp_in, near_in,
     bc_part, b_out, b_in, b_full, pay, pay_in, pay_all, pay_full, q_out, q_in, q_all, q_full,
     x_send, x_recv, s_send, s_recv, wx_sem, e_sem, in_sem,
@@ -155,44 +156,55 @@
     dout_load.start()
     pl.semaphore_wait(barrier, NT - 1 + NDP - 1)
 
-    def x_copy(way, to, src, half):
-        part = xall.at[src, pl.ds(half * HALF, HALF)]
+    def x_copy(way, to, src, part):
+        here = xall.at[src, pl.ds(part * QUARTER, QUARTER)]
         return pltpu.make_async_remote_copy(
-            src_ref=part,
-            dst_ref=part,
-            send_sem=x_send.at[way, src, half],
-            recv_sem=x_recv.at[src, half],
+            src_ref=here,
+            dst_ref=here,
+            send_sem=x_send.at[way, src, part],
+            recv_sem=x_recv.at[src, part],
             device_id={"tensor": to},
             device_id_type=MESH,
         )
 
     sent = []
 
-    def send(way, to, src, half):
-        copy = x_copy(way, to, src, half)
+    def send(way, to, src, part):
+        copy = x_copy(way, to, src, part)
         copy.start()
         sent.append(copy)
 
-    def send_own(way, to, half):
-        rows = pl.ds(half * HALF, HALF)
+    def send_own(way, to, part):
+        rows = pl.ds(part * QUARTER, QUARTER)
         copy = pltpu.make_async_remote_copy(
             src_ref=x_hbm.at[rows],
             dst_ref=xall.at[me, rows],
-            send_sem=x_send.at[way, me, half],
-            recv_sem=x_recv.at[me, half],
+            send_sem=x_send.at[way, me, part],
+            recv_sem=x_recv.at[me, part],
             device_id={"tensor": to},
             device_id_type=MESH,
         )
         copy.start()
         sent.append(copy)
 
-    def arrive(src, half):
-        x_copy(0, zp, src, half).wait_recv()
-
-    for half in range(2):
-        send_own(0, zp, half)
-        send_own(1, zm, 1 - half)
-        send_own(2, xp, half)
+    def arrive(src, part):
+        x_copy(0, zp, src, part).wait_recv()
+
+    def pass_far(part):
+        arrive(zm, part)
+        send(0, zp, zm, part)
+        arrive(zp, part + 2)
+        send(1, zm, zp, part + 2)
+
+    def pass_across(part):
+        arrive(xp, part)
+        send(0, zp, xp, part)
+        send(1, zm, xp, part)
+
+    for part in range(4):
+        send_own(0, zp, part)
+        send_own(1, zm, (part + 2) % 4)
+        send_own(2, xp, part)
 
     step = softplus(dt_ref[...])
     rate = head_rates(alog_ref) * step
@@ -215,18 +227,16 @@
         both = dot_nt(q_two, e_hi)
         eq_ref[:, b * CH : (b + 1) * CH] = both[:RANK] + both[RANK:] + dot_nt(q_hi, e_lo)
 
-    for b in range(5):
+    for b in range(3):
         e_block(b)
-
-    arrive(zm, 0)
-    send(0, zp, zm, 0)
-    arrive(zp, 1)
-    send(1, zm, zp, 1)
-    arrive(xp, 0)
-    send(0, zp, xp, 0)
-    send(1, zm, xp, 0)
+    pass_far(0)
+    for b in range(3, 5):
+        e_block(b)
+    pass_far(1)
+    pass_across(0)
     for b in range(5, NT):
         e_block(b)
+    pass_across(1)
 
     def weights(h, carry):
         cum_row = cum_ref[pl.ds(h, 1), :]
@@ -245,16 +255,13 @@
                     wt_mat[h, here, there] = (scores_t[here, there] * jnp.exp(span)).astype(BF16)
         return carry
 
-    lax.fori_loop(0, HEADS, weights, 0)
-
-    arrive(xp, 1)
-    send(0, zp, xp, 1)
-    send(1, zm, xp, 1)
+    lax.fori_loop(0, HEADS // 2, weights, 0)
+    pass_across(2)
+    lax.fori_loop(HEADS // 2, HEADS, weights, 0)
+    pass_across(3)
 
     for b in range(NT):
         wx_copy(b).wait()
-    arrive(zm, 1)
-    arrive(zp, 0)
 
     def product(src):
         rows = pl.ds(pl.multiple_of(src * CH, CH), CH)
@@ -262,18 +269,23 @@
 
     own_load.wait()
     acc[...] = product(me) + product(xp)
-    acc[...] += product(zm) + product(zp)
-    arrive(zo, 0)
-    send(2, xp, zo, 0)
-    arrive(zo, 1)
-    send(2, xp, zo, 1)
+    for part in range(2):
+        arrive(zo, part)
+        send(2, xp, zo, part)
+        arrive(zo, part + 2)
+        send(2, xp, zo, part + 2)
+        if part == 0:
+            for half in range(2):
+                arrive(zm, half + 2)
+                arrive(zp, half)
+            acc[...] += product(zm) + product(zp)
     acc[...] += product(zo)
     xp_zp = ((z + 1) % 4) * 2 + (1 - xl)
     xp_zm = ((z + 3) % 4) * 2 + (1 - xl)
     xp_zo = ((z + 2) % 4) * 2 + (1 - xl)
     for other in (xp_zp, xp_zm, xp_zo):
-        arrive(other, 0)
-        arrive(other, 1)
+        for part in range(4):
+            arrive(other, part)
         acc[...] += product(other)
     inner_ref[...] = acc[...].astype(BF16)
     gate_load.wait()
@@ -489,6 +501,7 @@
     head_back(1)
     merge(0)
     merge(1)
+    merge(2)
     for k in range(1, 4):
         y_copy(k).wait_recv()
     for c in range(2):
@@ -496,36 +509,46 @@
     low_copy = remote(p_low.at[1 - xh], x_in, low_sem.at[0], low_sem.at[1], "dp", other_x)
     begin(low_copy)
 
+    head_back(2)
+    merge(3)
+    merge(4)
+    mine = core * 8 + place
+    low_copy.wait_recv()
+    p_full[mine] = (p_low[xh] + x_in[...]) / NDP
+
+    def g_copy(chunk, to, n):
+        return remote(
+            p_full.at[chunk], p_full.at[chunk], g_send.at[n], g_recv.at[chunk], "dp", to
+        )
+
+    begin(g_copy(mine, other_x, 0))
+    for k in (2, 1, 3):
+        begin(g_copy(mine, y_peer(k), k))
+    begin(g_copy(mine, other_core, 4))
+
     dx_copy(0).wait_recv()
     opposite = input_part(zo) + dx_in[0].astype(F32)
     for i in range(2):
         opp_out[i] = opposite[i * HALF : (i + 1) * HALF].astype(BF16)
         begin(opp_copy(i))
 
-    head_back(2)
-    mine = core * 8 + place
-    low_copy.wait_recv()
-    p_full[mine] = (p_low[xh] + x_in[...]) / NDP
-
-    def g_copy(chunk, to, n):
-        return remote(
-            p_full.at[chunk], p_full.at[chunk], g_send.at[n], g_recv.at[chunk], "dp", to
-        )
-
-    begin(g_copy(mine, other_x, 0))
-    for k in (2, 1, 3):
-        begin(g_copy(mine, y_peer(k), k))
-    begin(g_copy(mine, other_core, 4))
-
-    def gram_one(c):
-        three = jnp.concatenate(split3(p_full[c]), axis=0)
-        p_three[c] = three
-        g9 = dot_nt(three, three)
-        g3 = g9[:RANK] + g9[RANK : 2 * RANK] + g9[2 * RANK :]
-        grams[c] = g3[:, :RANK] + g3[:, RANK : 2 * RANK] + g3[:, 2 * RANK :]
-
-    gram_one(mine)
+    def prepare(c):
+        p_three[c] = jnp.concatenate(split3(p_full[c]), axis=0)
+
+    def fold(c):
+        rows = pl.ds(pl.multiple_of(c * 256, 256), 256)
+        three = p_three[c]
+        high = dot_nn(three, m_hi[rows, :])
+        low = dot_nn(three[: 2 * RANK], m_lo[rows, :])
+        s_acc[...] += (
+            high[:RANK] + high[RANK : 2 * RANK] + high[2 * RANK :] + low[:RANK] + low[RANK:]
+        )
+
+    prepare(mine)
     head_back(3)
+    for s in range(5, NT):
+        merge(s)
+    s_acc[...] = jnp.zeros((RANK, CH), F32)
 
     bc_part[:, :128] = dot_nn(d_scores[...].T.astype(BF16), c_part)
     bc_part[:, 128:] = dot_nn(d_scores[...].astype(BF16), b_part)
@@ -545,7 +568,9 @@
         input_part(xp) + part_in[0].astype(F32) + part_in[1].astype(F32)
     ).astype(BF16)
     begin(dx_copy(1))
-    gram_one(across_x)
+    prepare(across_x)
+    fold(mine)
+    fold(across_x)
 
     lower = (iota((T, T), 0) >= iota((T, T), 1)).astype(F32)
     columns = col_sum[...]
@@ -563,49 +588,91 @@
         pay.at[pl.ds((1 - core) * 8, 8)], pay_in, pay_sem.at[0], pay_sem.at[1], "dp", other_core
     )
     begin(pay_core)
-    for s in range(2, 5):
-        merge(s)
-
-    for k in (1, 3, 2):
-        for c in range(2):
-            chunk = core * 8 + ((y + k) % 4) * 2 + c
-            g_copy(chunk, other_core, 0).wait_recv()
-            begin(g_copy(chunk, other_core, 7 + 2 * k + c))
-            gram_one(chunk)
-
-    pay_core.wait_recv()
-    pay_all[place] = pay[pl.ds(core * 8, 8), :] + pay_in[...]
-
-    def pay_copy(k, slot):
-        return remote(
-            pay_all.at[slot], pay_all.at[slot], ys_sem.at[k], yr_sem.at[k], "dp", same_core(k)
-        )
-
-    for k in FAR:
-        begin(pay_copy(k, place))
-
+
+    def take(chunk):
+        g_copy(chunk, other_core, 0).wait_recv()
+        prepare(chunk)
+        fold(chunk)
+
+    their = (1 - core) * 8
+    for c in range(2):
+        take(their + y * 2 + c)
+    near_chunks = [
+        (core * 8 + ((y + k) % 4) * 2 + c, 7 + 2 * k + c) for k in (1, 3, 2) for c in range(2)
+    ]
+    for chunk, n in near_chunks:
+        g_copy(chunk, other_core, 0).wait_recv()
+        begin(g_copy(chunk, other_core, n))
+    for chunk, n in near_chunks:
+        prepare(chunk)
+        fold(chunk)
     for i in range(2):
         rows = slice(i * HALF, (i + 1) * HALF)
         opp_copy(i).wait_recv()
         near_out[i, rows] = (near_hold[i] + opp_in[i].astype(F32)).astype(BF16)
         begin(near_copy(i, i))
 
+    for k in (1, 3, 2):
+        for c in range(2):
+            take(their + ((y + k) % 4) * 2 + c)
+
+    for c in range(2):
+        q_out[c] = s_acc[c * 16 : (c + 1) * 16]
+    q_core = remote(q_out.at[1 - core], q_in, q_sem.at[0], q_sem.at[1], "dp", other_core)
+    begin(q_core)
+
     def b_copy(k):
         to = (me + k) % NT
         return remote(b_out.at[to], b_in.at[k], bs_sem.at[k], br_sem.at[k], "tensor", to)
 
     loop(NT, lambda k: b_copy(k).start())
-    for s in range(5, NT):
-        merge(s)
-
-    for c in range(8):
-        chunk = (1 - core) * 8 + c
-        g_copy(chunk, other_core, 0).wait_recv()
-        gram_one(chunk)
-
-    gram = grams[0]
-    for c in range(1, NDP):
-        gram = gram + grams[c]
+
+    def gram_add(c, total):
+        three = p_three[c]
+        return total + dot_nt(three, three)
+
+    g9 = jnp.zeros((3 * RANK, 3 * RANK), F32)
+    for c in range(NDP):
+        g9 = gram_add(c, g9)
+    g3 = g9[:RANK] + g9[RANK : 2 * RANK] + g9[2 * RANK :]
+    gram = g3[:, :RANK] + g3[:, RANK : 2 * RANK] + g3[:, 2 * RANK :]
+
+    q_core.wait_recv()
+    q_all[place] = q_out[core] + q_in[...]
+
+    def q_copy(k, slot):
+        return remote(
+            q_all.at[slot], q_all.at[slot], qs_sem.at[k], qr_sem.at[k], "dp", same_core(k)
+        )
+
+    for k in FAR:
+        begin(q_copy(k, place))
+
+    pay_core.wait_recv()
+    pay_all[place] = pay[pl.ds(core * 8, 8), :] + pay_in[...]
+
+    def pay_copy(k, slot):
+        return remote(
+            pay_all.at[slot], pay_all.at[slot], ys_sem.at[k], yr_sem.at[k], "dp", same_core(k)
+        )
+
+    for k in FAR:
+        begin(pay_copy(k, place))
+
+    def b_add(k, total):
+        b_copy(k).wait_recv()
+        return total + b_in[k].astype(F32)
+
+    my_rows = pl.ds(pl.multiple_of(me * rows_each, 16), rows_each)
+    b_full[me] = lax.fori_loop(1, NT, b_add, bc_part[my_rows, :]).astype(BF16)
+
+    def c_copy(k, slot):
+        return remote(
+            b_full.at[slot], b_full.at[slot], cs_sem.at[k], cr_sem.at[k], "tensor", (me + k) % NT
+        )
+
+    loop(NT, lambda k: c_copy(k, me).start())
+
     eye = (iota((RANK, RANK), 0) == iota((RANK, RANK), 1)).astype(F32)
     table = jnp.concatenate([eye, gram], axis=1)
     places = iota((RANK, 2 * RANK), 0)
@@ -627,49 +694,24 @@
         ],
         axis=0,
     )
-    q_local = jnp.zeros((RANK, CH), F32)
-    for s in range(NT):
-        blocks = []
-        for c in (2 * s, 2 * s + 1):
-            three = dot_nn(left, p_three[c])
-            blocks.append(three[:RANK] + three[RANK : 2 * RANK] + three[2 * RANK :])
-        ph = jnp.concatenate(blocks, axis=1)
-        rows = slice(s * CH, (s + 1) * CH)
-        ph_ref[:, rows] = ph
-        hi, lo = split2(ph)
-        both = dot_nn(jnp.concatenate([hi, lo], axis=0), m_hi[rows])
-        q_local = q_local + both[:RANK] + both[RANK:] + dot_nn(hi, m_lo[rows])
-
-    for c in range(2):
-        q_out[c] = q_local[c * 16 : (c + 1) * 16]
-    q_core = remote(q_out.at[1 - core], q_in, q_sem.at[0], q_sem.at[1], "dp", other_core)
-    begin(q_core)
-    q_core.wait_recv()
-    q_all[place] = q_out[core] + q_in[...]
-
-    def q_copy(k, slot):
-        return remote(
-            q_all.at[slot], q_all.at[slot], qs_sem.at[k], qr_sem.at[k], "dp", same_core(k)
-        )
-
-    for k in FAR:
-        begin(q_copy(k, place))
-
-    def b_add(k, total):
-        b_copy(k).wait_recv()
-        return total + b_in[k].astype(F32)
-
-    my_rows = pl.ds(pl.multiple_of(me * rows_each, 16), rows_each)
-    b_full[me] = lax.fori_loop(1, NT, b_add, bc_part[my_rows, :]).astype(BF16)
-
-    def c_copy(k, slot):
-        return remote(
-            b_full.at[slot], b_full.at[slot], cs_sem.at[k], cr_sem.at[k], "tensor", (me + k) % NT
-        )
-
-    loop(NT, lambda k: c_copy(k, me).start())
-
-    total = input_part(me)
+    for c in range(NDP):
+        three = dot_nn(left, p_three[c])
+        ph_ref[:, c * 256 : (c + 1) * 256] = (
+            three[:RANK] + three[RANK : 2 * RANK] + three[2 * RANK :]
+        )
+
+    acc[...] = input_part(me)
+    for k in range(1, 8):
+        q_copy(k, (place + 8 - k) % 8).wait_recv()
+    q_sum = q_all[0]
+    for c in range(1, 8):
+        q_sum = q_sum + q_all[c]
+    q_full[core] = q_sum
+    q_back = remote(
+        q_full.at[core], q_full.at[core], q_sem.at[2], q_sem.at[3], "dp", other_core
+    )
+    begin(q_back)
+
     for i in range(2):
         for half in range(2):
             near_copy(i, half).wait_recv()
@@ -677,20 +719,9 @@
     for half in range(2):
         rows = slice(half * HALF, (half + 1) * HALF)
         dinp_ref[rows] = (
-            total[rows] + near_in[0, half].astype(F32) + near_in[1, half].astype(F32)
+            acc[rows] + near_in[0, half].astype(F32) + near_in[1, half].astype(F32)
             + dx_in[1, rows].astype(F32)
         ).astype(BF16)
-
-    for k in range(1, 8):
-        q_copy(k, (place + 8 - k) % 8).wait_recv()
-    q_sum = q_all[0]
-    for c in range(1, 8):
-        q_sum = q_sum + q_all[c]
-    q_full[core] = q_sum / NDP
-    q_back = remote(
-        q_full.at[core], q_full.at[core], q_sem.at[2], q_sem.at[3], "dp", other_core
-    )
-    begin(q_back)
 
     for k in range(1, 8):
         pay_copy(k, (place + 8 - k) % 8).wait_recv()
@@ -713,8 +744,10 @@
     ).wait_recv()
     for c in range(2):
         pay_ref[c * 8 : (c + 1) * 8] = pay_full[c]
-    for c in range(2):
-        qm_ref[c * 16 : (c + 1) * 16] = q_full[c]
+    s_sum = jnp.concatenate([q_full[0], q_full[1]], axis=0)
+    qm_ref[...] = (
+        jnp.dot(inverse, s_sum, precision=HIGH, preferred_element_type=F32) / NDP
+    )
 
     for copy in sent:
         copy.wait_send()
@@ -835,7 +868,7 @@
             pltpu.VMEM((RANK, 256), F32),
             pltpu.VMEM((NDP, RANK, 256), F32),
             pltpu.VMEM((NDP, 3 * RANK, 256), BF16),
-            pltpu.VMEM((NDP, RANK, RANK), F32),
+            pltpu.VMEM((RANK, CH), F32),
             pltpu.VMEM((D, CH), BF16),
             pltpu.VMEM((D, CH), BF16),
             pltpu.VMEM((2, T, CH), BF16),
@@ -859,7 +892,7 @@
             pltpu.VMEM((RANK // 2, CH), F32),
             pltpu.VMEM((8, RANK // 2, CH), F32),
             pltpu.VMEM((2, RANK // 2, CH), F32),
-            DMA((3, NT, 2)), DMA((NT, 2)), DMA((NT,)), DMA((NT,)), DMA((NT,)), DMA((NT,)), DMA((3,)),
+            DMA((3, NT, 4)), DMA((NT, 4)), DMA((NT,)), DMA((NT,)), DMA((NT,)), DMA((NT,)), DMA((3,)),
             DMA((2,)), DMA((4,)), DMA((4,)), DMA((2,)), DMA((16,)), DMA((NDP,)),
             DMA((2,)), DMA((2,)), DMA((2,)), DMA((2,)), DMA((2,)), DMA((2,)), DMA((2, 2)), DMA((2, 2)),
             DMA((NT,)), DMA((NT,)), DMA((NT,)), DMA((NT,)),

time: 87.4 us -> 85.2 us (0.975)
  Pallas kernels: 86.7 us -> 84.4 us
    pallas_call x1, Pallas kernels: 81.8 us -> 79.6 us  [shards(): pl.pallas_call(main_kernel, name='main', out_shape=(pltpu.VMEM((D, CH), F...]
where the time goes in v4:
time: 85.2 us; the launch traced here: 85.1 us
  Pallas kernels  84.4 us (99%)
    pallas_call x1, Pallas kernels, shards(): pl.pallas_call(main_kernel, name='main', out_shape=(pltpu.VMEM((D, CH), F...  79.6 us
    pallas_call x1, Pallas kernels, shards(): pl.pallas_call(error_kernel, name='error', grid=(D // ROWS,), out_shape=(...  4.87 us

profile of v4, /device:TPU:1, one launch (start us, length us, event | category | flops | bytes accessed | tf_op | source)
XLA Modules:
  0.0 85.1 jit_solution(236766991840370155)
XLA Ops:
  0.6 79.6 %main.1 = (f32[4096,512]{1,0:T(8,128)S(1)}, f32[32,4096]{1,0:T(8,128)S(1)}, f32[32,512]{1,0:T(8,128)S(1)}, bf16[384,512]{1,0:T(8,128)(2,1)S(1)}, f32[384,256]{1,...) custom-call(bf16[384,512]{1,0:T(8,128)(2,1)} %x_hbm.1, ...), custom_call_target="tpu_custom_call" | custom-call | tf_op jit(solution)/shard_map/main/pallas_call | solution.py:829
  80.2 4.9 %error.1 = (f32[4096,512]{1,0:T(8,128)}, f32[32,4096]{1,0:T(8,128)}, f32[32,512]{1,0:T(8,128)}, bf16[384,512]{1,0:T(8,128)(2,1)}, f32[384,256]{1,0:T(8,128)}, /*...) custom-call(f32[4096,512]{1,0:T(8,128)S(1)} %get-tuple-element.28.m_ref, ...), custom_call_target="tpu_custom_call" | custom-call | tf_op jit(solution)/shard_map/error/pallas_call | solution.py:913
